TPU v7x, 256 devices: a whole 4x4x8 slice. The times are simulated.
256 devices in a mesh: dp: 32 (over y, z_hi, core), seq: 8 (over x, z_lo).
Axes of the slice: x: 4, y: 4, z: 8 (z_hi: 4, z_lo: 2; z = z_hi * 2 + z_lo), core: 2. Of those that a mesh axis runs over, the one named last changes fastest.
Arguments:
- qkv_spatial: bfloat16 [32, 16, 64, 3456], P('dp', 'seq'), may hold values from -52 to 52
- tokens: bfloat16 [32, 16, 64, 1152], P('dp', 'seq'), may hold values from -6 to 6
- timesteps: int32 [32], P('dp'), may hold values from 0 to 999
- w_spatial_out: bfloat16 [1152, 1152], P('dp'), may hold values from -0.1875 to 0.1875
- w_temporal_in: bfloat16 [1152, 3456], P('dp'), may hold values from -0.26516504 to 0.26516504
- grad_out: bfloat16 [32, 16, 64, 1152], P('dp', None, 'seq'), may hold values from -2 to 2
Outputs:
- grad_qkv_spatial: bfloat16 [32, 16, 64, 3456], P('dp', 'seq')
- grad_tokens: bfloat16 [32, 16, 64, 1152], P('dp', 'seq')
- grad_w_spatial_out: float32 [1152, 1152], P('dp', 'seq')
- grad_w_temporal_in: float32 [1152, 3456], P('dp', 'seq')
All inputs are finite; a program needn't handle non-finite values.
Results may differ from a plain program's by a relative error of at most 0.025.
Values may be sent and summed in bfloat16 or wider, within the bound.
A program may use at most 128 MiB of HBM per device.

v0:
```python
import math

import jax
import jax.numpy as jnp
from jax import lax
from jax.sharding import PartitionSpec as P

HEADS = 16


def attention_core(packed):
    group_count, positions, packed_width = packed.shape
    head_size = packed_width // (3 * HEADS)
    pieces = packed.astype(jnp.float32).reshape(group_count, positions, 3, HEADS, head_size)
    queries = pieces[:, :, 0]
    key_part = pieces[:, :, 1]
    value_part = pieces[:, :, 2]
    scores = jnp.einsum("gshe,gthe->ghst", queries, key_part, precision=lax.Precision.HIGHEST) * (
        1.0 / math.sqrt(head_size)
    )
    probs = jax.nn.softmax(scores, axis=-1)
    rounded = lax.optimization_barrier(probs.astype(jnp.bfloat16)).astype(jnp.float32)
    attended = jnp.einsum("ghst,gthe->gshe", rounded, value_part, precision=lax.Precision.HIGHEST)
    return attended.reshape(group_count, positions, HEADS * head_size).astype(jnp.bfloat16)


def time_modulation(timesteps, model_width):
    half_width = model_width // 2
    frequency = jnp.exp(-math.log(10000.0) * jnp.arange(half_width, dtype=jnp.float32) / half_width)
    angles = timesteps.astype(jnp.float32)[:, None] * frequency[None, :]
    cosine = jnp.cos(angles)
    sine = jnp.sin(angles)
    scales = 0.5 * jnp.concatenate([cosine, sine], axis=-1)
    shifts = 0.5 * jnp.concatenate([sine, cosine], axis=-1)
    return (scales, shifts)


def modulate(field_in, scales, shifts):
    values_f = field_in.astype(jnp.float32)
    row_mean = jnp.mean(values_f, axis=-1, keepdims=True)
    centred = values_f - row_mean
    row_var = jnp.mean(centred * centred, axis=-1, keepdims=True)
    return centred * lax.rsqrt(row_var + 1e-06) * (1.0 + scales) + shifts


def shards(qkv_spatial, tokens, timesteps, w_spatial_out, w_temporal_in, grad_out):
    samples, frame_count, patches, packed_width = qkv_spatial.shape
    model_width = packed_width // 3
    whole_out, whole_in = (
        lax.all_gather(w_spatial_out, "dp", axis=0, tiled=True),
        lax.all_gather(w_temporal_in, "dp", axis=0, tiled=True),
    )
    spatial_flat = qkv_spatial.reshape(samples * frame_count, patches, packed_width)
    mixed_out, pull_spatial = jax.vjp(attention_core, spatial_flat)
    mixed_rows = mixed_out.reshape(-1, model_width)
    hidden = (
        tokens.reshape(-1, model_width).astype(jnp.float32)
        + jnp.dot(mixed_rows, whole_out, preferred_element_type=jnp.float32)
    ).astype(jnp.bfloat16)
    hidden = hidden.reshape(samples, frame_count, patches, model_width)
    patch_hidden = lax.all_to_all(hidden, "seq", split_axis=2, concat_axis=1, tiled=True)
    frames = patch_hidden.shape[1]
    local_patches = patch_hidden.shape[2]
    scales, shifts = time_modulation(timesteps, model_width)

    def norm_field(field_in):
        return modulate(field_in, scales[:, None, :], shifts[:, None, :])

    modulated, pull_norm = jax.vjp(
        norm_field, patch_hidden.reshape(samples, frames * local_patches, model_width)
    )
    modulated_rows = modulated.astype(jnp.bfloat16).reshape(-1, model_width)
    qkv_temporal = jnp.dot(modulated_rows, whole_in, preferred_element_type=jnp.float32).astype(
        jnp.bfloat16
    )
    temporal_flat = (
        qkv_temporal.reshape(samples, frames, local_patches, packed_width)
        .transpose(0, 2, 1, 3)
        .reshape(samples * local_patches, frames, packed_width)
    )
    unused_out, pull_temporal = jax.vjp(attention_core, temporal_flat)
    cotangent = grad_out.transpose(0, 2, 1, 3).reshape(samples * local_patches, frames, model_width)
    (grad_flat,) = pull_temporal(cotangent)
    grad_temporal = (
        grad_flat.reshape(samples, local_patches, frames, packed_width)
        .transpose(0, 2, 1, 3)
        .reshape(-1, packed_width)
    )
    temporal_cols = lax.all_to_all(grad_temporal, "seq", split_axis=1, concat_axis=0, tiled=True)
    grad_modulated = jnp.dot(grad_temporal, whole_in.T, preferred_element_type=jnp.float32)
    (grad_hidden,) = pull_norm(grad_modulated.reshape(samples, frames * local_patches, model_width))
    grad_hidden = grad_hidden.reshape(samples, frames, local_patches, model_width)
    frame_grad = lax.all_to_all(grad_hidden, "seq", split_axis=1, concat_axis=2, tiled=True)
    grad_rows = frame_grad.reshape(-1, model_width)
    spatial_cols = lax.all_to_all(grad_rows, "seq", split_axis=1, concat_axis=0, tiled=True)
    grad_mixed = jnp.dot(grad_rows, whole_out.T, preferred_element_type=jnp.float32).astype(
        jnp.bfloat16
    )
    (grad_spatial,) = pull_spatial(grad_mixed.reshape(samples * frame_count, patches, model_width))
    spatial_sum = lax.dot_general(
        lax.all_gather(mixed_rows, "seq", axis=0, tiled=True),
        spatial_cols,
        (((0,), (0,)), ((), ())),
        preferred_element_type=jnp.float32,
    )
    temporal_sum = lax.dot_general(
        lax.all_gather(modulated_rows, "seq", axis=0, tiled=True),
        temporal_cols,
        (((0,), (0,)), ((), ())),
        preferred_element_type=jnp.float32,
    )
    partials = (
        lax.psum_scatter(
            spatial_sum.astype(jnp.bfloat16), "dp", scatter_dimension=0, tiled=True
        ).astype(jnp.float32),
        lax.psum_scatter(
            temporal_sum.astype(jnp.bfloat16), "dp", scatter_dimension=0, tiled=True
        ).astype(jnp.float32),
    )
    return (grad_spatial.reshape(qkv_spatial.shape), frame_grad, partials[0], partials[1])


def solution(mesh):
    placed = (
        P("dp", "seq", None, None),
        P("dp", "seq", None, None),
        P("dp"),
        P("dp", None),
        P("dp", None),
        P("dp", None, "seq", None),
    )
    return jax.shard_map(
        shards,
        mesh=mesh,
        in_specs=placed,
        out_specs=(
            P("dp", "seq", None, None),
            P("dp", "seq", None, None),
            P("dp", "seq"),
            P("dp", "seq"),
        ),
        check_vma=False,
    )
```

profile of v0, /device:TPU:50, one launch (start us, length us, event | category | flops | bytes accessed | tf_op | source)
XLA Modules:
  0.0 418.7 jit_solution(7120420433081204091)
XLA Ops:
  8.7 4.0 reshape.328
  18.2 50.3 %all-gather.11.cloned.1.call-done = bf16[32,36,1152]{2,1,0:T(8,128)(2,1)} async-done(((bf16[1,36,1152]{2,1,0:T(8,128)(2,1)}), bf16[32,36,1152]{2,1,0:T(8,128)(2,1)}) %all-gather.11.cloned.1.call-update) | async-done | bytes 2654224 | tf_op jit(solution)/shard_map/all_gather | solution.py:50
  68.5 3.6 reshape.343
  73.8 5.7 %all-to-all-start = ((bf16[1,2,64,1152]{3,1,0,2:T(2,128)(2,1)}), bf16[1,2,64,1152]{3,1,0,2:T(2,128)(2,1)S(1)}, u32[]{:S(2)}, u32[]{:S(2)}) async-start(bf16[1,2,64,1152]{3,1,0,2:T(2,128)(2,1)} %copy.153), calls=%async_computation | async-start | bytes 589824 | tf_op jit(solution)/shard_map/all_to_all | solution.py:61
  80.1 2.8 reshape.332
  88.0 62.6 %all-gather.13.cloned.1.call-done = bf16[32,36,3456]{2,1,0:T(8,128)(2,1)} async-done(((bf16[1,36,3456]{2,1,0:T(8,128)(2,1)}), bf16[32,36,3456]{2,1,0:T(8,128)(2,1)}) %all-gather.13.cloned.1.call-update) | async-done | bytes 7962640 | tf_op jit(solution)/shard_map/all_gather | solution.py:51
  150.6 12.4 %reshape.345 = bf16[1152,3456]{1,0:T(8,128)(2,1)} reshape(bf16[32,36,3456]{2,1,0:T(8,128)(2,1)} %all-gather.13.cloned.1.call-done) | data formatting | bytes 15925248
  163.0 4.6 %fusion.4 = bf16[1,16,8,3456]{3,2,1,0:T(8,128)(2,1)S(1)} fusion(bf16[128,1152]{1,0:T(8,128)(2,1)S(1)} %copy-done.8, bf16[1152,3456]{1,0:T(8,128)(2,1)} %reshape.345), kind=kOutput, calls=%fused_computation.3 | convolution fusion | flops 1019658240 | bytes 9142272 | tf_op jit(solution)/shard_map/dot_general | solution.py:73
  168.6 4.7 %reshape.331 = bf16[8,16,3,16,72]{4,3,2,1,0:T(8,128)(2,1)} reshape(bf16[1,8,16,3456]{3,2,1,0:T(8,128)(2,1)} %bitcast.171) | data formatting | bytes 1769472 | tf_op jit(solution)/shard_map/jvp()/reshape | solution.py:14
  175.4 4.1 fusion.52
  185.0 3.8 convert_element_type.160
  188.8 6.2 %multiply_reduce_fusion = (f32[128]{0:T(128)S(1)}, f32[128,1152]{1,0:T(8,128)S(1)}) fusion(f32[1,2,8,8,1152]{4,3,1,2,0:T(8,128)S(1)} %copy.154, f32[128]{0:T(128)S(1)} %copy-done.20, f32[1152]{0:T(1024)S(1)} %copy-done.17, bf16[1152,3456]{1,0:T(8,128)(2,1)} %reshape.345, bf16[1,16,8,3456]{3,1,2,0:T(8,128)(2,1)} %bitcast.169), kind=kOutput, calls=%fused_computation.55 | convolution fusion | flops 1019805568 | bytes 10032640 | tf_op jit(solution)/shard_map/dot_general | solution.py:90
  195.4 15.3 %all_to_all.65 = bf16[1,16,8,1152]{3,2,0,1:T(8,128)(2,1)S(1)} all-to-all(bf16[1,16,8,1152]{3,2,0,1:T(8,128)(2,1)S(1)} %fusion.35), channel_id=1, replica_groups=mesh['dp'=32,'seq'=8] {'seq'}, dimensions={1} | all-to-all | bytes 589824 | tf_op jit(solution)/shard_map/all_to_all | solution.py:93
  211.5 2.5 all_to_all.53
  213.9 2.1 copy.173
  216.1 6.2 %all-to-all-start.2 = ((bf16[128,8,144]{0,2,1:T(8,128)(2,1)}), bf16[128,8,144]{0,2,1:T(8,128)(2,1)}, u32[]{:S(2)}, u32[]{:S(2)}) async-start(bf16[128,8,144]{0,2,1:T(8,128)(2,1)} %copy.173), calls=%async_computation.2 | async-start | bytes 589824 | tf_op jit(solution)/shard_map/all_to_all | solution.py:95
  225.9 4.3 %all_to_all.57 = bf16[128,8,432]{2,1,0:T(8,128)(2,1)} reshape(bf16[1,16,8,3456]{3,2,1,0:T(8,128)(2,1)} %copy.164) | data formatting | bytes 1769472 | tf_op jit(solution)/shard_map/all_to_all | solution.py:89
  230.2 2.6 copy.176
  232.8 5.8 %all-to-all-start.3 = ((bf16[128,8,432]{0,2,1:T(8,128)(2,1)}), bf16[128,8,432]{0,2,1:T(8,128)(2,1)}, u32[]{:S(2)}, u32[]{:S(2)}) async-start(bf16[128,8,432]{0,2,1:T(8,128)(2,1)} %copy.176), calls=%async_computation.3 | async-start | bytes 1769472 | tf_op jit(solution)/shard_map/all_to_all | solution.py:89
  240.3 2.0 reshape.336
  244.3 2.1 convolution_bitcast_fusion.2
  248.2 2.5 convolution_convert_fusion.2
  250.7 31.2 %all-gather.9.cloned.1.call-done = bf16[1024,1152]{1,0:T(8,128)(2,1)} async-done(((bf16[128,1152]{1,0:T(8,128)(2,1)}), bf16[1024,1152]{1,0:T(8,128)(2,1)}) %all-gather.9.cloned.1.call-update) | async-done | bytes 2359312 | tf_op jit(solution)/shard_map/all_gather | solution.py:107
  281.9 3.3 convolution_convert_fusion.1
  285.2 75.0 %fusion.47 = (bf16[40,144]{1,0:T(8,128)(2,1)S(1)}, bf16[40,432]{1,0:T(8,128)(2,1)S(1)}) fusion(bf16[1152,144]{1,0:T(8,128)(2,1)S(1)} %convolution_convert_fusion.2, bf16[1152,432]{1,0:T(8,128)(2,1)S(1)} %convolution_convert_fusion.1), kind=kCustom, calls=%all-reduce-scatter.2 | all-reduce-scatter fusion | flops 737281 | bytes 1374208
  366.0 9.2 %collective-permute-start.3 = (bf16[4,144]{1,0:T(4,128)(2,1)S(1)}, bf16[4,144]{1,0:T(4,128)(2,1)S(1)}, u32[]{:S(2)}, u32[]{:S(2)}) collective-permute-start(bf16[4,144]{1,0:T(4,128)(2,1)S(1)} %slice.30), channel_id=1, source_target_pairs={{0,32},{8,40},{16,48},{24,56},{32,64},{40,72},{48,80},{56,88},{64,... | collective-permute-start | bytes 3464
  375.3 2.0 add_convert_fusion
  378.2 2.6 convert_element_type.166
  380.9 8.7 %collective-permute-start.6 = (bf16[40,432]{1,0:T(8,128)(2,1)S(1)}, bf16[40,432]{1,0:T(8,128)(2,1)S(1)}, u32[]{:S(2)}, u32[]{:S(2)}) collective-permute-start(bf16[40,432]{1,0:T(8,128)(2,1)S(1)} %get-tuple-element.7), channel_id=1, source_target_pairs={{0,24},{8,32},{16,40},{24,48},{32,56},{40,64},{48,72},{56,80},{64,... | collective-permute-start | bytes 103688
  389.6 9.0 %collective-permute-start.5 = (bf16[40,432]{1,0:T(8,128)(2,1)S(1)}, bf16[40,432]{1,0:T(8,128)(2,1)S(1)}, u32[]{:S(2)}, u32[]{:S(2)}) collective-permute-start(bf16[40,432]{1,0:T(8,128)(2,1)S(1)} %get-tuple-element.7), channel_id=1, source_target_pairs={{0,16},{8,24},{16,32},{24,40},{32,48},{40,56},{48,64},{56,72},{64,... | collective-permute-start | bytes 103688
  400.6 2.2 collective-permute-start.7
  404.0 6.9 %collective-permute-done.7 = bf16[4,432]{1,0:T(4,128)(2,1)S(1)} collective-permute-done((bf16[4,432]{1,0:T(4,128)(2,1)S(1)}, bf16[4,432]{1,0:T(4,128)(2,1)S(1)}, u32[]{:S(2)}, u32[]{:S(2)}) %collective-permute-start.7) | collective-permute-done | bytes 3488
  (125 shorter events, 42.8 us)
Async XLA Ops:
  7.2 61.4 %all-gather.11.cloned.1.call-start = ((), (), s32[]{:S(2)}) async-start(), calls=%async_computation.6 | async-start | bytes 3041280 | tf_op jit(solution)/shard_map/all_gather | solution.py:50
  7.9 142.7 %all-gather.13.cloned.1.call-start = ((), (), s32[]{:S(2)}) async-start(), calls=%async_computation.7 | async-start | bytes 9123840 | tf_op jit(solution)/shard_map/all_gather | solution.py:51
  8.6 239.6 %all-gather.7.cloned.1.call-start = ((), (), s32[]{:S(2)}) async-start(), calls=%async_computation.4 | async-start | bytes 2654208 | tf_op jit(solution)/shard_map/all_gather | solution.py:101
  13.0 3.2 copy-start.12
  13.0 3.2 copy-start.14
  13.0 3.2 copy-start.3
  18.2 53.9 %copy-start.10 = (bf16[128,1152]{1,0:T(8,128)(2,1)S(1)}, bf16[128,1152]{1,0:T(8,128)(2,1)}, u32[]{:S(2)}) copy-start(bf16[128,1152]{1,0:T(8,128)(2,1)} %convert_element_type.143) | copy-start | bytes 884740
  18.2 53.9 %copy-start.16 = (bf16[1,2,64,1152]{3,2,1,0:T(8,128)(2,1)S(1)}, bf16[1,2,64,1152]{3,2,1,0:T(8,128)(2,1)}, u32[]{:S(2)}) copy-start(bf16[1,2,64,1152]{3,2,1,0:T(8,128)(2,1)} %param.7) | copy-start | bytes 884740
  73.8 11.7 %all-to-all-start = ((bf16[1,2,64,1152]{3,1,0,2:T(2,128)(2,1)}), bf16[1,2,64,1152]{3,1,0,2:T(2,128)(2,1)S(1)}, u32[]{:S(2)}, u32[]{:S(2)}) async-start(bf16[1,2,64,1152]{3,1,0,2:T(2,128)(2,1)} %copy.153), calls=%async_computation | async-start | bytes 589824 | tf_op jit(solution)/shard_map/all_to_all | solution.py:61
  79.5 202.4 %all-gather.9.cloned.1.call-start = ((), (), s32[]{:S(2)}) async-start(), calls=%async_computation.5 | async-start | bytes 2654208 | tf_op jit(solution)/shard_map/all_gather | solution.py:107
  88.0 75.0 %copy-start.8 = (bf16[128,1152]{1,0:T(8,128)(2,1)S(1)}, bf16[128,1152]{1,0:T(8,128)(2,1)}, u32[]{:S(2)}) copy-start(bf16[128,1152]{1,0:T(8,128)(2,1)} %add_convert_fusion.3) | copy-start | bytes 884740
  175.0 4.5 %copy-start.7 = (bf16[8,16,16,72]{3,2,0,1:T(8,128)(2,1)S(1)}, bf16[8,16,16,72]{3,2,0,1:T(8,128)(2,1)}, u32[]{:S(2)}) copy-start(bf16[8,16,16,72]{3,2,0,1:T(8,128)(2,1)} %reshape.332) | copy-start | bytes 884740
  183.4 5.4 %copy-start.17 = (f32[1152]{0:T(1024)S(1)}, f32[1152]{0:T(1024)}, u32[]{:S(2)}) copy-start(f32[1152]{0:T(1024)} %get-tuple-element.21) | copy-start | bytes 13828
  183.4 5.4 %copy-start.20 = (f32[128]{0:T(128)S(1)}, f32[128]{0:T(128)}, u32[]{:S(2)}) copy-start(f32[128]{0:T(128)} %copy-done.19) | copy-start | bytes 1540
  188.8 6.2 %copy-start.24 = (f32[128]{0:T(128)S(1)}, f32[128]{0:T(128)}, u32[]{:S(2)}) copy-start(f32[128]{0:T(128)} %copy-done.23) | copy-start | bytes 1540
  188.8 6.2 %copy-start.22 = (f32[128]{0:T(128)S(1)}, f32[128]{0:T(128)}, u32[]{:S(2)}) copy-start(f32[128]{0:T(128)} %copy-done.21) | copy-start | bytes 1540
  195.3 29.5 %copy-start.2 = (bf16[1,8,16,3456]{3,2,1,0:T(8,128)(2,1)S(1)}, bf16[1,8,16,3456]{3,2,1,0:T(8,128)(2,1)}, u32[]{:S(2)}) copy-start(bf16[1,8,16,3456]{3,2,1,0:T(8,128)(2,1)} %convert_element_type.160) | copy-start | bytes 2654212
  216.1 16.7 %all-to-all-start.2 = ((bf16[128,8,144]{0,2,1:T(8,128)(2,1)}), bf16[128,8,144]{0,2,1:T(8,128)(2,1)}, u32[]{:S(2)}, u32[]{:S(2)}) async-start(bf16[128,8,144]{0,2,1:T(8,128)(2,1)} %copy.173), calls=%async_computation.2 | async-start | bytes 589824 | tf_op jit(solution)/shard_map/all_to_all | solution.py:95
  225.9 12.7 %copy-start.11 = (bf16[1,2,8,8,1152]{4,3,2,1,0:T(8,128)(2,1)S(1)}, bf16[1,2,8,8,1152]{4,3,2,1,0:T(8,128)(2,1)}, u32[]{:S(2)}) copy-start(bf16[1,2,8,8,1152]{4,3,2,1,0:T(8,128)(2,1)} %copy.244) | copy-start | bytes 884740
  232.8 9.5 %copy-start.4 = (bf16[2,64,1,16,72]{4,3,2,1,0:T(8,128)(2,1)S(1)}, bf16[2,64,1,16,72]{4,3,2,1,0:T(8,128)(2,1)}, u32[]{:S(2)}) copy-start(bf16[2,64,1,16,72]{4,3,2,1,0:T(8,128)(2,1)} %copy-done.3) | copy-start | bytes 884740
  232.8 49.2 %all-to-all-start.3 = ((bf16[128,8,432]{0,2,1:T(8,128)(2,1)}), bf16[128,8,432]{0,2,1:T(8,128)(2,1)}, u32[]{:S(2)}, u32[]{:S(2)}) async-start(bf16[128,8,432]{0,2,1:T(8,128)(2,1)} %copy.176), calls=%async_computation.3 | async-start | bytes 1769472 | tf_op jit(solution)/shard_map/all_to_all | solution.py:89
  238.6 4.1 copy-start.18
  240.3 2.7 copy-start.6
  250.7 124.5 %copy-start.9 = (f32[2,64,1,16,72]{4,1,3,0,2:T(8,128)S(1)}, f32[2,64,1,16,72]{4,1,3,0,2:T(8,128)}, u32[]{:S(2)}) copy-start(f32[2,64,1,16,72]{4,1,3,0,2:T(8,128)} %convolution_bitcast_fusion) | copy-start | bytes 1769476
  360.3 38.4 %collective-permute-start.2 = (bf16[40,144]{1,0:T(8,128)(2,1)S(1)}, bf16[40,144]{1,0:T(8,128)(2,1)S(1)}, u32[]{:S(2)}, u32[]{:S(2)}) collective-permute-start(bf16[40,144]{1,0:T(8,128)(2,1)S(1)} %get-tuple-element.6), channel_id=1, source_target_pairs={{0,24},{8,32},{16,40},{24,48},{32,56},{40,64},{48,72},{56,80},{64,... | collective-permute-start | bytes 34568
  362.2 38.4 %collective-permute-start.1 = (bf16[40,144]{1,0:T(8,128)(2,1)S(1)}, bf16[40,144]{1,0:T(8,128)(2,1)S(1)}, u32[]{:S(2)}, u32[]{:S(2)}) collective-permute-start(bf16[40,144]{1,0:T(8,128)(2,1)S(1)} %get-tuple-element.6), channel_id=1, source_target_pairs={{0,16},{8,24},{16,32},{24,40},{32,48},{40,56},{48,64},{56,72},{64,... | collective-permute-start | bytes 34568
  364.1 38.7 %collective-permute-start = (bf16[40,144]{1,0:T(8,128)(2,1)S(1)}, bf16[40,144]{1,0:T(8,128)(2,1)S(1)}, u32[]{:S(2)}, u32[]{:S(2)}) collective-permute-start(bf16[40,144]{1,0:T(8,128)(2,1)S(1)} %get-tuple-element.6), channel_id=1, source_target_pairs={{0,8},{8,16},{16,24},{24,32},{32,40},{40,48},{48,56},{56,64},{64,7... | collective-permute-start | bytes 34568
  366.0 23.6 %collective-permute-start.3 = (bf16[4,144]{1,0:T(4,128)(2,1)S(1)}, bf16[4,144]{1,0:T(4,128)(2,1)S(1)}, u32[]{:S(2)}, u32[]{:S(2)}) collective-permute-start(bf16[4,144]{1,0:T(4,128)(2,1)S(1)} %slice.30), channel_id=1, source_target_pairs={{0,32},{8,40},{16,48},{24,56},{32,64},{40,72},{48,80},{56,88},{64,... | collective-permute-start | bytes 3464
  380.9 30.1 %collective-permute-start.6 = (bf16[40,432]{1,0:T(8,128)(2,1)S(1)}, bf16[40,432]{1,0:T(8,128)(2,1)S(1)}, u32[]{:S(2)}, u32[]{:S(2)}) collective-permute-start(bf16[40,432]{1,0:T(8,128)(2,1)S(1)} %get-tuple-element.7), channel_id=1, source_target_pairs={{0,24},{8,32},{16,40},{24,48},{32,56},{40,64},{48,72},{56,80},{64,... | collective-permute-start | bytes 103688
  389.6 21.3 %collective-permute-start.5 = (bf16[40,432]{1,0:T(8,128)(2,1)S(1)}, bf16[40,432]{1,0:T(8,128)(2,1)S(1)}, u32[]{:S(2)}, u32[]{:S(2)}) collective-permute-start(bf16[40,432]{1,0:T(8,128)(2,1)S(1)} %get-tuple-element.7), channel_id=1, source_target_pairs={{0,16},{8,24},{16,32},{24,40},{32,48},{40,56},{48,64},{56,72},{64,... | collective-permute-start | bytes 103688
  398.7 12.3 %collective-permute-start.4 = (bf16[40,432]{1,0:T(8,128)(2,1)S(1)}, bf16[40,432]{1,0:T(8,128)(2,1)S(1)}, u32[]{:S(2)}, u32[]{:S(2)}) collective-permute-start(bf16[40,432]{1,0:T(8,128)(2,1)S(1)} %get-tuple-element.7), channel_id=1, source_target_pairs={{0,8},{8,16},{16,24},{24,32},{32,40},{40,48},{48,56},{56,64},{64,7... | collective-permute-start | bytes 103688
  400.6 10.3 %collective-permute-start.7 = (bf16[4,432]{1,0:T(4,128)(2,1)S(1)}, bf16[4,432]{1,0:T(4,128)(2,1)S(1)}, u32[]{:S(2)}, u32[]{:S(2)}) collective-permute-start(bf16[4,432]{1,0:T(4,128)(2,1)S(1)} %slice.31), channel_id=1, source_target_pairs={{0,32},{8,40},{16,48},{24,56},{32,64},{40,72},{48,80},{56,88},{64,... | collective-permute-start | bytes 10376
  (8 other events, 14.7 us)
Sparse Core Ops, SparseCore 0:
  10.6 57.8 all-gather.10
  71.1 79.4 all-gather.12
  152.4 59.5 all-gather.6
  213.6 68.3 all-gather.8
where the time goes:
time: 420 us; the launch traced here: 419 us
  waiting for transfers between devices  154 us (37%)
  blocking collectives  90.3 us (22%)
  local copies, waits for them, and re-layouts  61.1 us (15%)
  starting transfers between devices  54.7 us (13%)
  matrix products  28.6 us (7%)
  between operations  15.7 us (4%)
  other arithmetic  14 us (3%)
    unnamed x1, blocking collectives  75 us
    all_gather x1, waiting for transfers between devices, shards(): lax.all_gather(w_temporal_in, 'dp', axis=0, tiled=True)  62.6 us
    all_gather x1, waiting for transfers between devices, shards(): lax.all_gather(w_spatial_out, 'dp', axis=0, tiled=True)  50.3 us
    unnamed x8, starting transfers between devices  36.8 us
    all_gather x1, waiting for transfers between devices, shards(): lax.all_gather(modulated_rows, 'seq', axis=0, tiled=True)  31.2 us
    unnamed x57, local copies, waits for them, and re-layouts  19.6 us
    all_to_all x1, blocking collectives, shards(): lax.all_to_all(grad_hidden, 'seq', split_axis=1, concat_axis=2, tiled=True)  15.3 us
    convert_element_type x4, local copies, waits for them, and re-layouts, attention_core(): packed.astype(jnp.float32)  9.02 us
  transfers between devices with their start and end apart: 15, of which 5 were waited for; matrix products, arithmetic and copies ran while one was open for 22% of the time, Pallas kernels for 0%

commit v1 on v0

v1 whole, which is shorter than its diff:
```python
import functools
import math

import jax
import jax.numpy as jnp
from jax import lax
from jax.experimental import pallas as pl
from jax.experimental.pallas import tpu as pltpu
from jax.sharding import PartitionSpec as P

HEADS = 16
D = 1152
HEAD = D // HEADS
T = 128
NY, NZ, NC, NS = 4, 4, 2, 8
NX = 4
SHARD = 36
MAIN, TAIL = 32, 4
BLOCK = NZ * SHARD
CHUNKS = 4
F32, BF = jnp.float32, jnp.bfloat16
MESH = pl.DeviceIdType.MESH
SCALE = 1.0 / math.sqrt(HEAD)
VMEM = pltpu.VMEM
DMA = pltpu.SemaphoreType.DMA


def contract(a, b, da, db):
    return lax.dot_general(a, b, (((da,), (db,)), ((), ())), preferred_element_type=F32)


def regroup(block):
    return jnp.concatenate(
        [block[64 * f + 8 * p : 64 * f + 8 * p + 8] for p in range(8) for f in range(2)], axis=0
    )


def ungroup(block):
    return jnp.concatenate(
        [block[16 * p + 8 * f : 16 * p + 8 * f + 8] for f in range(2) for p in range(8)], axis=0
    )


def lanes(i, n=128):
    return pl.ds(pl.multiple_of(i * n, 128), n)


def rows8(start, n):
    return pl.ds(pl.multiple_of(start, 8), n)


def loop(n, body, unroll=1):
    lax.fori_loop(0, n, lambda i, c: (body(i), c)[1], 0, unroll=unroll)


def rows_to_t(src, dst, n, group=False):
    def body(j):
        x = src[:, lanes(j)].astype(F32)
        if group:
            x = regroup(x)
        dst[rows8(j * 128, 128), :] = x.T.astype(dst.dtype)

    loop(n // 128, body)


def t_to_rows(src, dst, n):
    def body(j):
        dst[:, lanes(j)] = src[rows8(j * 128, 128), :].T.astype(dst.dtype)

    loop(n // 128, body)


def permute(src, dst):
    def body(y):
        x = src[rows8(y * 288, 288), :]
        parts = []
        for c in range(NC):
            parts += [x[72 * z + 36 * c : 72 * z + 36 * c + 32] for z in range(NZ)]
            parts += [x[72 * z + 36 * c + 32 : 72 * z + 36 * c + 36] for z in range(NZ)]
        dst[rows8(y * 288, 288), :] = jnp.concatenate(parts, axis=0)

    loop(NY, body)


def unpermute(src, dst):
    def body(y):
        x = src[rows8(y * 288, 288), :]
        parts = []
        for z in range(NZ):
            for c in range(NC):
                parts.append(x[144 * c + 32 * z : 144 * c + 32 * z + 32])
                parts.append(x[144 * c + 128 + 4 * z : 144 * c + 128 + 4 * z + 4])
        dst[rows8(y * 288, 288), :] = jnp.concatenate(parts, axis=0)

    loop(NY, body)


def head_slices(ref, h):
    return [ref[rows8(D * i + HEAD * h, HEAD), :].astype(BF) for i in range(3)]


def attend(packed, bias, probs, out):
    def body(h):
        for hh in (2 * h, 2 * h + 1):
            q = packed[rows8(HEAD * hh, HEAD), :].astype(BF)
            k = packed[rows8(D + HEAD * hh, HEAD), :].astype(BF)
            s = contract(k, q, 0, 0) * SCALE + bias[...]
            e = jnp.exp(s - jnp.max(s, axis=0, keepdims=True))
            p = e / jnp.sum(e, axis=0, keepdims=True)
            probs[hh] = p
            if out is not None:
                v = packed[rows8(2 * D + HEAD * hh, HEAD), :].astype(BF)
                o = contract(v, p.astype(BF), 1, 0)
                out[rows8(HEAD * hh, HEAD), :] = o.astype(BF).astype(F32)

    loop(HEADS // 2, body)


def attend_back(packed, probs, cot, grad):
    def body(h):
        for hh in (2 * h, 2 * h + 1):
            q, k, v = head_slices(packed, hh)
            do = cot[rows8(HEAD * hh, HEAD), :].astype(BF)
            p = probs[hh]
            dp = contract(v, do, 0, 0).astype(BF).astype(F32)
            dv = contract(do, p.astype(BF), 1, 1)
            ds = p * (dp - jnp.sum(dp * p, axis=0, keepdims=True)) * SCALE
            ds = ds.astype(BF)
            dq = contract(k, ds, 1, 0)
            dk = contract(q, ds, 1, 1)
            grad[rows8(HEAD * hh, HEAD), :] = dq
            grad[rows8(D + HEAD * hh, HEAD), :] = dk
            grad[rows8(2 * D + HEAD * hh, HEAD), :] = dv

    loop(HEADS // 2, body)


def kernel(
    qkv, tokens, gout, wo, wi, tail, sc, sh,
    out_qkv, out_tok, out_gwo, out_gwi,
    w, tails, packed, spat, probs, probs_t, bias, grad, grad_b, ft, fp, rows_b, rows_t, hid, hid_in, g_out,
    xhat, rstd, mixed_all, mod_all, gt_all, g_all, cot, g_in, gt_b,
    gwi_y, gwo_y, gwi_yin, gwo_yin, gwi_z, gwo_z, gwi_zin, gwo_zin,
    z_s, z_r, t_s, t_r, y_s, y_r, c_s, c_r, mx_s, mx_r, md_s, md_r,
    h_s, h_r, g_s, g_r, gt_s, gt_r, gc_s, gc_r, ri_s, ri_r, ro_s, ro_r, si_s, si_r, so_s, so_r,
):
    d = lax.axis_index("dp")
    s = lax.axis_index("seq")
    y, u = d // 8, d % 8
    z, c = u // 2, u % 2
    x, zl = s // 2, s % 2
    mine = y * 2 + c

    def z_peer(k):
        return (y * 8 + lax.rem(z + k, NZ) * 2 + c, s)

    def y_peer(k):
        return (lax.rem(y + k, NY) * 8 + u, s)

    core_peer = (d + 1 - 2 * c, s)

    def u_peer(k):
        return (y * 8 + lax.rem(u + k, 8), s)

    def x_peer(k):
        return (d, lax.rem(x + k, NX) * 2 + zl)

    pair = (d, s + 1 - 2 * zl)

    def s_peer(k):
        return (d, lax.rem(s + k, NS))

    peers = (
        [z_peer(k) for k in range(1, NZ)]
        + [y_peer(k) for k in range(1, NY)]
        + [u_peer(k) for k in range(1, 8)]
        + [s_peer(k) for k in range(1, NS)]
    )
    peers = peers[3:]
    barrier = pltpu.get_barrier_semaphore()
    for p in peers:
        pl.semaphore_signal(barrier, inc=1, device_id=p, device_id_type=MESH)

    started = []

    def copy(src, dst, ss, rs, to):
        return pltpu.make_async_remote_copy(
            src_ref=src, dst_ref=dst, send_sem=ss, recv_sem=rs, device_id=to, device_id_type=MESH
        )

    def go(cp):
        cp.start()
        started.append(cp)

    def w_main(q):
        if q == 0:
            return wo.at[pl.ds(0, MAIN), :]
        return wi.at[pl.ds(0, MAIN), pl.ds((q - 1) * D, D)]

    def z_copy(q, k):
        return copy(
            w_main(q), w.at[q, mine, pl.ds(pl.multiple_of(z * MAIN, 16), MAIN), :],
            z_s.at[q, k - 1], z_r.at[q, k - 1], z_peer(k),
        )

    def t_copy(k):
        return copy(tail, tails.at[z], t_s.at[k - 1], t_r.at[k - 1], z_peer(k))

    def y_copy(q, k):
        return copy(w.at[q, mine], w.at[q, mine], y_s.at[q, k - 1], y_r.at[q, k - 1], y_peer(k))

    def c_copy(q, k):
        blk = lax.rem(y + NY - k, NY) * 2 + c
        return copy(w.at[q, blk], w.at[q, blk], c_s.at[q, k], c_r.at[q, k], core_peer)

    def gather_pair(buf, ss, rs):
        return copy(buf.at[:, lanes(s)], buf.at[:, lanes(s)], ss.at[0], rs.at[0], pair)

    def gather_x(buf, ss, rs, k, other):
        slot = s + (1 - 2 * zl) * other
        i = k + 3 * other
        return copy(buf.at[:, lanes(slot)], buf.at[:, lanes(slot)], ss.at[i], rs.at[i], x_peer(k))

    def rows_copy(src, dst, ss, rs, k):
        to = lax.rem(s + k, NS)
        return copy(
            src.at[pl.ds(pl.multiple_of(to * 16, 16), 16), :],
            dst.at[pl.ds(pl.multiple_of(s * 16, 16), 16), :],
            ss.at[k - 1], rs.at[k - 1], s_peer(k),
        )

    def cols_copy(src, dst, n, ss, rs, k):
        to = lax.rem(s + k, NS)
        return copy(
            src.at[pl.ds(pl.multiple_of(to * n, 16), n), :], dst.at[:, lanes(s)],
            ss.at[k - 1], rs.at[k - 1], s_peer(k),
        )

    def sum_y(src, dst, ss, rs, k):
        return copy(src.at[lax.rem(y + k, NY)], dst.at[k - 1], ss.at[k - 1], rs.at[k - 1], y_peer(k))

    def sum_z(src, dst, ss, rs, k):
        return copy(src.at[lax.rem(u + k, 8)], dst.at[k - 1], ss.at[k - 1], rs.at[k - 1], u_peer(k))

    for q in range(CHUNKS):
        w[q, mine, pl.ds(pl.multiple_of(z * MAIN, 16), MAIN), :] = w_main(q)[...]
    tails[z] = tail[...]
    pl.semaphore_wait(barrier, len(peers))

    for k in range(1, NZ):
        go(t_copy(k))
    for q in range(CHUNKS):
        for k in range(1, NZ):
            go(z_copy(q, k))

    rows_to_t(qkv, spat, 3 * D, group=True)
    ki = lax.broadcasted_iota(jnp.int32, (T, T), 0)
    qi = lax.broadcasted_iota(jnp.int32, (T, T), 1)
    bias[...] = jnp.where((ki // 8) % 2 == (qi // 8) % 2, 0.0, -1e30).astype(F32)
    attend(spat, bias, probs, ft)
    mixed_all[:, lanes(s)] = ft[...].astype(BF)
    go(gather_pair(mixed_all, mx_s, mx_r))
    permute(ft, fp)
    t_to_rows(fp, rows_b, D)
    bias[...] = jnp.where(ki % 8 == qi % 8, 0.0, -1e30).astype(F32)
    rows_to_t(gout, cot, D)

    for k in range(1, NZ):
        t_copy(k).wait_recv()

    low = lax.broadcasted_iota(jnp.int32, (8, 128), 0) < 4

    def tail_body(m):
        full = [tails[zz, pl.ds(pl.multiple_of(m * 16, 16), 16), :].astype(F32) for zz in range(NZ)]
        for half in range(2):
            a = [v[8 * half : 8 * half + 8] for v in full]
            r = [pltpu.roll(v, 4, 0) for v in a]
            even = [jnp.where(low, a[0], r[1]), jnp.where(low, a[2], r[3])]
            odd = [jnp.where(low, r[0], a[1]), jnp.where(low, r[2], a[3])]
            for i, pieces in enumerate((even, odd)):
                j = 4 * m + 2 * half + i
                w[j // 9, mine, pl.ds(NZ * MAIN, 16), lanes(j % 9)] = jnp.concatenate(pieces, axis=0).astype(BF)

    loop(9, tail_body)

    def spread(q):
        for k in range(1, NZ):
            z_copy(q, k).wait_recv()
        for k in range(1, NY):
            go(y_copy(q, k))
        go(c_copy(q, 0))

    def relay(q):
        for k in range(1, NY):
            y_copy(q, k).wait_recv()
            go(c_copy(q, k))

    def arrived(q):
        for k in range(NY):
            c_copy(q, k).wait_recv()

    def fan_out(buf, ss, rs):
        gather_pair(buf, ss, rs).wait_recv()
        for k in range(1, NX):
            go(gather_x(buf, ss, rs, k, 0))
            go(gather_x(buf, ss, rs, k, 1))

    def fanned(buf, ss, rs):
        for k in range(1, NX):
            gather_x(buf, ss, rs, k, 0).wait_recv()
            gather_x(buf, ss, rs, k, 1).wait_recv()

    spread(0)
    fan_out(mixed_all, mx_s, mx_r)
    spread(1)
    relay(0)
    arrived(0)

    def hidden_body(n):
        tok = regroup(tokens[:, lanes(n, 384)].astype(F32))
        acc = contract(rows_b[...], w[0, :, :, lanes(n, 384)].reshape(D, 384), 1, 0)
        hid[:, lanes(n, 384)] = (tok + acc).astype(BF)

    loop(3, hidden_body)
    own = pl.ds(pl.multiple_of(s * 16, 16), 16)
    hid_in[own, :] = hid[own, :]
    for k in range(1, NS):
        go(rows_copy(hid, hid_in, h_s, h_r, k))
    spread(2)
    for k in range(1, NS):
        rows_copy(hid, hid_in, h_s, h_r, k).wait_recv()

    hf = hid_in[...].astype(F32)
    centred = hf - jnp.mean(hf, axis=-1, keepdims=True)
    inv = lax.rsqrt(jnp.mean(centred * centred, axis=-1, keepdims=True) + 1e-06)
    xh = centred * inv
    xhat[...] = xh
    rstd[...] = jnp.broadcast_to(inv, (T, 128))
    rows_t[...] = (xh * sc[...] + sh[...]).astype(BF).astype(F32)
    rows_to_t(rows_t, ft, D)
    mod_all[:, lanes(s)] = ft[...].astype(BF)
    go(gather_pair(mod_all, md_s, md_r))
    permute(ft, fp)
    t_to_rows(fp, rows_b, D)
    spread(3)
    fan_out(mod_all, md_s, md_r)

    def project(q):
        relay(q)
        arrived(q)

        def body(n):
            acc = contract(rows_b[...], w[q, :, :, lanes(n, 384)].reshape(D, 384), 1, 0)
            acc = acc.astype(BF).astype(F32)
            packed[rows8((q - 1) * D + n * 384, 384), :] = acc.T

        loop(3, body)

    project(1)
    project(2)
    attend(packed, bias, probs_t, None)
    project(3)
    attend_back(packed, probs_t, cot, grad)
    grad_b[...] = grad[...].astype(BF)
    gt_all[:, lanes(s)] = grad_b[pl.ds(pl.multiple_of(s * 432, 16), 432), :]
    for k in range(1, NS):
        go(cols_copy(grad_b, gt_all, 432, gt_s, gt_r, k))

    def back_body(b):
        acc = jnp.zeros((2 * BLOCK, T), F32)
        for q in range(1, CHUNKS):
            acc += contract(w[q, pl.ds(2 * b, 2)].reshape(2 * BLOCK, D), grad_b[pl.ds((q - 1) * D, D), :], 1, 0)
        fp[rows8(b * 2 * BLOCK, 2 * BLOCK), :] = acc

    loop(NY, back_body)
    unpermute(fp, ft)
    t_to_rows(ft, rows_t, D)
    dx = rows_t[...] * sc[...]
    xh = xhat[...]
    m1 = jnp.mean(dx, axis=-1, keepdims=True)
    m2 = jnp.mean(dx * xh, axis=-1, keepdims=True)
    g_out[...] = (rstd[:, 0:1] * (dx - m1 - xh * m2)).astype(BF)
    g_in[own, :] = g_out[own, :]
    for k in range(1, NS):
        go(rows_copy(g_out, g_in, g_s, g_r, k))
    for k in range(1, NS):
        rows_copy(g_out, g_in, g_s, g_r, k).wait_recv()

    def tok_body(j):
        v = g_in[:, lanes(j)].astype(F32)
        out_tok[:, lanes(j)] = ungroup(v).astype(BF)
        gt_b[rows8(j * 128, 128), :] = v.T.astype(BF)

    loop(9, tok_body)
    g_all[:, lanes(s)] = gt_b[pl.ds(pl.multiple_of(s * 144, 16), 144), :]
    for k in range(1, NS):
        go(cols_copy(gt_b, g_all, 144, gc_s, gc_r, k))

    def mixed_body(b):
        fp[rows8(b * 2 * BLOCK, 2 * BLOCK), :] = contract(
            w[0, pl.ds(2 * b, 2)].reshape(2 * BLOCK, D), gt_b[...], 1, 0
        )

    loop(NY, mixed_body)
    unpermute(fp, ft)

    fanned(mod_all, md_s, md_r)
    for k in range(1, NS):
        cols_copy(grad_b, gt_all, 432, gt_s, gt_r, k).wait_recv()

    def gwi_body(b):
        gwi_y[b] = contract(mod_all[rows8(b * 288, 288), :], gt_all[...], 1, 1).astype(BF)

    loop(NY, gwi_body)
    for k in range(1, NY):
        go(sum_y(gwi_y, gwi_yin, ri_s, ri_r, k))

    fanned(mixed_all, mx_s, mx_r)
    for k in range(1, NS):
        cols_copy(gt_b, g_all, 144, gc_s, gc_r, k).wait_recv()

    def gwo_body(b):
        gwo_y[b] = contract(mixed_all[rows8(b * 288, 288), :], g_all[...], 1, 1).astype(BF)

    loop(NY, gwo_body)
    for k in range(1, NY):
        go(sum_y(gwo_y, gwo_yin, ro_s, ro_r, k))

    def add_y(src, dst, ss, rs, out):
        for k in range(1, NY):
            sum_y(src, dst, ss, rs, k).wait_recv()
        acc = src[y].astype(F32)
        for k in range(1, NY):
            acc += dst[k - 1].astype(F32)
        for i in range(8):
            out[i, 0:SHARD, :] = acc[SHARD * i : SHARD * i + SHARD].astype(BF)
            out[i, SHARD:48, :] = jnp.zeros((48 - SHARD, acc.shape[1]), BF)

    def add_z(src, dst, ss, rs, out):
        for k in range(1, 8):
            sum_z(src, dst, ss, rs, k).wait_recv()
        acc = src[u].astype(F32)
        for k in range(1, 8):
            acc += dst[k - 1].astype(F32)
        out[...] = acc[0:SHARD]

    attend_back(spat, probs, ft, grad)
    add_y(gwi_y, gwi_yin, ri_s, ri_r, gwi_z)
    for k in range(1, 8):
        go(sum_z(gwi_z, gwi_zin, si_s, si_r, k))
    add_y(gwo_y, gwo_yin, ro_s, ro_r, gwo_z)
    for k in range(1, 8):
        go(sum_z(gwo_z, gwo_zin, so_s, so_r, k))

    def out_body(j):
        out_qkv[:, lanes(j)] = ungroup(grad[rows8(j * 128, 128), :].T).astype(BF)

    loop(27, out_body)
    add_z(gwi_z, gwi_zin, si_s, si_r, out_gwi)
    add_z(gwo_z, gwo_zin, so_s, so_r, out_gwo)
    for cp in started:
        cp.wait_send()


def time_modulation(timesteps):
    half = D // 2
    frequency = jnp.exp(-math.log(10000.0) * jnp.arange(half, dtype=F32) / half)
    angles = timesteps.astype(F32)[:, None] * frequency[None, :]
    cosine, sine = jnp.cos(angles), jnp.sin(angles)
    return (
        1.0 + 0.5 * jnp.concatenate([cosine, sine], axis=-1),
        0.5 * jnp.concatenate([sine, cosine], axis=-1),
    )


def shards(qkv_spatial, tokens, timesteps, w_out, w_in, grad_out):
    sc, sh = time_modulation(timesteps)
    tail = jnp.concatenate([w_out[MAIN:], w_in[MAIN:]], axis=1)
    tail = tail.reshape(TAIL, 36, 128).transpose(1, 0, 2).reshape(144, 128)
    dma = lambda *n: DMA(n)
    scratch = [
        VMEM((CHUNKS, NY * NC, BLOCK, D), BF),
        VMEM((NZ, 144, 128), BF),
        VMEM((3 * D, T), F32),
        VMEM((3 * D, T), F32),
        VMEM((HEADS, T, T), F32),
        VMEM((HEADS, T, T), F32),
        VMEM((T, T), F32),
        VMEM((3 * D, T), F32),
        VMEM((3 * D, T), BF),
        VMEM((D, T), F32),
        VMEM((D, T), F32),
        VMEM((T, D), BF),
        VMEM((T, D), F32),
        VMEM((T, D), BF),
        VMEM((T, D), BF),
        VMEM((T, D), BF),
        VMEM((T, D), F32),
        VMEM((T, 128), F32),
        VMEM((D, NS * T), BF),
        VMEM((D, NS * T), BF),
        VMEM((432, NS * T), BF),
        VMEM((144, NS * T), BF),
        VMEM((D, T), F32),
        VMEM((T, D), BF),
        VMEM((D, T), BF),
        VMEM((NY, 288, 432), BF),
        VMEM((NY, 288, 144), BF),
        VMEM((3, 288, 432), BF),
        VMEM((3, 288, 144), BF),
        VMEM((8, 48, 432), BF),
        VMEM((8, 48, 144), BF),
        VMEM((7, 48, 432), BF),
        VMEM((7, 48, 144), BF),
        dma(4, 3), dma(4, 3), dma(3), dma(3), dma(4, 3), dma(4, 3), dma(4, 4), dma(4, 4),
        dma(7), dma(7), dma(7), dma(7),
        dma(7), dma(7), dma(7), dma(7), dma(7), dma(7), dma(7), dma(7),
        dma(3), dma(3), dma(3), dma(3), dma(7), dma(7), dma(7), dma(7),
    ]
    spec = pl.BlockSpec(memory_space=VMEM)
    gq, gt, gwo, gwi = pl.pallas_call(
        kernel,
        out_shape=(
            jax.ShapeDtypeStruct((T, 3 * D), BF),
            jax.ShapeDtypeStruct((T, D), BF),
            jax.ShapeDtypeStruct((SHARD, 144), F32),
            jax.ShapeDtypeStruct((SHARD, 432), F32),
        ),
        in_specs=[spec] * 8,
        out_specs=(spec,) * 4,
        scratch_shapes=scratch,
        compiler_params=pltpu.CompilerParams(
            collective_id=0, has_side_effects=True, vmem_limit_bytes=60 * 1024 * 1024
        ),
    )(
        qkv_spatial.reshape(T, 3 * D), tokens.reshape(T, D), grad_out.reshape(T, D),
        w_out, w_in, tail, sc, sh,
    )
    return gq.reshape(qkv_spatial.shape), gt.reshape(tokens.shape), gwo, gwi


def solution(mesh):
    placed = (
        P("dp", "seq", None, None),
        P("dp", "seq", None, None),
        P("dp"),
        P("dp", None),
        P("dp", None),
        P("dp", None, "seq", None),
    )
    return jax.shard_map(
        shards,
        mesh=mesh,
        in_specs=placed,
        out_specs=(
            P("dp", "seq", None, None),
            P("dp", "seq", None, None),
            P("dp", "seq"),
            P("dp", "seq"),
        ),
        check_vma=False,
    )
```

time: 420 us -> 171 us (0.41)
  the two profiles are of different devices: /device:TPU:50 before, /device:TPU:1 now
where the time goes in v1:
time: 171 us
  Pallas kernels  163 us (95%)
  local copies, waits for them, and re-layouts  5.91 us (3%)
    pallas_call x1, Pallas kernels, shards(): pl.pallas_call(kernel, out_shape=(jax.ShapeDtypeStruct((T, 3 * D), BF), j...  163 us
    unnamed x10, local copies, waits for them, and re-layouts  4.5 us

profile of v1, /device:TPU:1, one launch (start us, length us, event | category | flops | bytes accessed | tf_op | source)
XLA Modules:
  0.0 170.9 jit_solution(11414917761127271027)
XLA Ops:
  1.4 0.7 maximum_multiply_fusion.1
  2.0 0.0 slice-start
  2.0 0.0 slice-start.1
  2.0 0.7 slice-done
  2.8 0.0 slice-done.1
  2.8 0.6 copy.11
  3.5 162.9 %shard_map.93 = (bf16[128,3456]{1,0:T(8,128)(2,1)}, bf16[128,1152]{1,0:T(8,128)(2,1)}, f32[36,144]{1,0:T(8,128)}, f32[36,432]{1,0:T(8,128)}) custom-call(bf16[128,3456]{1,0:T(8,128)(2,1)} %bitcast.8, bf16[128,1152]{1,0:T(8,128)(2,1)} %bitcast.10, bf16[128,1152]{1,0:T(8,128)(2,1)} %bitcast.11, bf16[36,1152]{1,0:T(8,128)(2,1)} %wo.1, bf16[36,3456]{1,0:T(8,128)(2,1)} %wi.1, ...), custom_call_target="tpu_custom_call" | custom-call | tf_op jit(solution)/shard_map/pallas_call | solution.py:521
  166.4 0.0 copy-start
  166.4 2.2 %copy.17 = bf16[1,2,64,3456]{3,2,1,0:T(8,128)(2,1)} copy(bf16[1,2,64,3456]{3,2,1,0:T(8,128)(2,1)} %bitcast.9) | data formatting | bytes 1769472
  168.6 0.0 copy-done
  168.6 0.0 copy-start.2
  168.6 0.7 copy.18
  169.3 0.1 copy-done.2
  169.4 0.0 copy-start.1
  169.4 0.6 copy.19
  170.0 0.3 copy-done.1
  170.3 0.6 copy.20
  (5 shorter events, 0.1 us)
Async XLA Ops:
  2.0 0.7 slice-start
  2.0 0.7 slice-start.1
  166.4 2.2 %copy-start = (bf16[128,1152]{1,0:T(8,128)(2,1)S(1)}, bf16[128,1152]{1,0:T(8,128)(2,1)}, u32[]{:S(2)}) copy-start(bf16[128,1152]{1,0:T(8,128)(2,1)} %get-tuple-element.9) | copy-start | bytes 884740
  168.6 0.8 copy-start.2
  169.4 0.9 copy-start.1

commit v2 on v1

--- a/solution.py
+++ b/solution.py
@@ -73,23 +73,22 @@
 def permute(src, dst):
     def body(y):
         x = src[rows8(y * 288, 288), :]
-        parts = []
         for c in range(NC):
-            parts += [x[72 * z + 36 * c : 72 * z + 36 * c + 32] for z in range(NZ)]
+            parts = [x[72 * z + 36 * c : 72 * z + 36 * c + 32] for z in range(NZ)]
             parts += [x[72 * z + 36 * c + 32 : 72 * z + 36 * c + 36] for z in range(NZ)]
-        dst[rows8(y * 288, 288), :] = jnp.concatenate(parts, axis=0)
+            dst[rows8(576 * c + y * 144, 144), :] = jnp.concatenate(parts, axis=0)
 
     loop(NY, body)
 
 
 def unpermute(src, dst):
     def body(y):
-        x = src[rows8(y * 288, 288), :]
+        x = [src[rows8(576 * c + y * 144, 144), :] for c in range(NC)]
         parts = []
         for z in range(NZ):
             for c in range(NC):
-                parts.append(x[144 * c + 32 * z : 144 * c + 32 * z + 32])
-                parts.append(x[144 * c + 128 + 4 * z : 144 * c + 128 + 4 * z + 4])
+                parts.append(x[c][32 * z : 32 * z + 32])
+                parts.append(x[c][128 + 4 * z : 128 + 4 * z + 4])
         dst[rows8(y * 288, 288), :] = jnp.concatenate(parts, axis=0)
 
     loop(NY, body)
@@ -116,8 +115,9 @@
     loop(HEADS // 2, body)
 
 
-def attend_back(packed, probs, cot, grad):
+def attend_back(packed, probs, cot, grad, first=0, count=HEADS):
     def body(h):
+        h = h + first // 2
         for hh in (2 * h, 2 * h + 1):
             q, k, v = head_slices(packed, hh)
             do = cot[rows8(HEAD * hh, HEAD), :].astype(BF)
@@ -132,7 +132,7 @@
             grad[rows8(D + HEAD * hh, HEAD), :] = dk
             grad[rows8(2 * D + HEAD * hh, HEAD), :] = dv
 
-    loop(HEADS // 2, body)
+    loop(count // 2, body)
 
 
 def kernel(
@@ -140,16 +140,16 @@
     out_qkv, out_tok, out_gwo, out_gwi,
     w, tails, packed, spat, probs, probs_t, bias, grad, grad_b, ft, fp, rows_b, rows_t, hid, hid_in, g_out,
     xhat, rstd, mixed_all, mod_all, gt_all, g_all, cot, g_in, gt_b,
-    gwi_y, gwo_y, gwi_yin, gwo_yin, gwi_z, gwo_z, gwi_zin, gwo_zin,
+    gwi_p, gwi_c, gwi_h, gwi_y, gwi_t, gwi_z, gwo_p, gwo_c, gwo_h, gwo_y, gwo_t, gwo_z,
     z_s, z_r, t_s, t_r, y_s, y_r, c_s, c_r, mx_s, mx_r, md_s, md_r,
-    h_s, h_r, g_s, g_r, gt_s, gt_r, gc_s, gc_r, ri_s, ri_r, ro_s, ro_r, si_s, si_r, so_s, so_r,
+    h_s, h_r, g_s, g_r, gt_s, gt_r, gc_s, gc_r, ri_s, ri_r, ro_s, ro_r,
 ):
     d = lax.axis_index("dp")
     s = lax.axis_index("seq")
     y, u = d // 8, d % 8
     z, c = u // 2, u % 2
     x, zl = s // 2, s % 2
-    mine = y * 2 + c
+    mine = c * NY + y
 
     def z_peer(k):
         return (y * 8 + lax.rem(z + k, NZ) * 2 + c, s)
@@ -206,20 +206,31 @@
     def t_copy(k):
         return copy(tail, tails.at[z], t_s.at[k - 1], t_r.at[k - 1], z_peer(k))
 
-    def y_copy(q, k):
-        return copy(w.at[q, mine], w.at[q, mine], y_s.at[q, k - 1], y_r.at[q, k - 1], y_peer(k))
-
-    def c_copy(q, k):
-        blk = lax.rem(y + NY - k, NY) * 2 + c
-        return copy(w.at[q, blk], w.at[q, blk], c_s.at[q, k], c_r.at[q, k], core_peer)
-
-    def gather_pair(buf, ss, rs):
-        return copy(buf.at[:, lanes(s)], buf.at[:, lanes(s)], ss.at[0], rs.at[0], pair)
-
-    def gather_x(buf, ss, rs, k, other):
-        slot = s + (1 - 2 * zl) * other
-        i = k + 3 * other
-        return copy(buf.at[:, lanes(slot)], buf.at[:, lanes(slot)], ss.at[i], rs.at[i], x_peer(k))
+    def block(k):
+        return c * NY + lax.rem(y + NY + k, NY)
+
+    def y_copy(q, i):
+        part = w.at[q, mine]
+        if i == 2:
+            part = w.at[q, block(-1), pl.ds(0, 80), :]
+        if i == 3:
+            part = w.at[q, block(1), pl.ds(80, 64), :]
+        return copy(part, part, y_s.at[q, i], y_r.at[q, i], y_peer(1 if i % 2 == 0 else 3))
+
+    def c_copy(q, i):
+        part = w.at[q, block((0, -1, 1, 2)[i])]
+        return copy(part, part, c_s.at[q, i], c_r.at[q, i], core_peer)
+
+    def gather_copy(buf, ss, rs, i):
+        if i == 0:
+            part, to = buf.at[:, lanes(s)], pair
+        elif i < 3:
+            part, to = buf.at[:, lanes(x, 256)], x_peer(1 if i == 1 else 3)
+        elif i == 3:
+            part, to = buf.at[:, lanes(2 * lax.rem(x + 3, NX))], x_peer(1)
+        else:
+            part, to = buf.at[:, lanes(2 * lax.rem(x + 1, NX) + 1)], x_peer(3)
+        return copy(part, part, ss.at[i], rs.at[i], to)
 
     def rows_copy(src, dst, ss, rs, k):
         to = lax.rem(s + k, NS)
@@ -236,11 +247,59 @@
             ss.at[k - 1], rs.at[k - 1], s_peer(k),
         )
 
-    def sum_y(src, dst, ss, rs, k):
-        return copy(src.at[lax.rem(y + k, NY)], dst.at[k - 1], ss.at[k - 1], rs.at[k - 1], y_peer(k))
-
-    def sum_z(src, dst, ss, rs, k):
-        return copy(src.at[lax.rem(u + k, 8)], dst.at[k - 1], ss.at[k - 1], rs.at[k - 1], u_peer(k))
+    def sum_c(part, got, ss, rs):
+        return copy(
+            part.at[:, pl.ds(pl.multiple_of((1 - c) * 144, 16), 144), :], got, ss.at[0], rs.at[0], core_peer
+        )
+
+    def sum_y(half, got, ss, rs, k):
+        return copy(half.at[lax.rem(y + k, NY)], got.at[k - 1], ss.at[k], rs.at[k], y_peer(k))
+
+    def sum_z(slab, got, ss, rs, j):
+        return copy(slab.at[j], got.at[z], ss.at[4 + j], rs.at[4 + z], (y * 8 + 4 * c + j, s))
+
+    def add_c(part, got, half, ygot, ss, rs):
+        sum_c(part, got, ss, rs).wait_recv()
+
+        def body(b):
+            own_half = part[b, pl.ds(pl.multiple_of(c * 144, 16), 144), :].astype(F32)
+            half[b] = (own_half + got[b].astype(F32)).astype(BF)
+
+        loop(NY, body)
+        for k in range(1, NY):
+            go(sum_y(half, ygot, ss, rs, k))
+
+    def add_y(half, got, slab, zgot, ss, rs):
+        for k in range(1, NY):
+            sum_y(half, got, ss, rs, k).wait_recv()
+        acc = half[y].astype(F32)
+        for k in range(1, NY):
+            acc += got[k - 1].astype(F32)
+        for j in range(4):
+            slab[j, 0:SHARD, :] = acc[SHARD * j : SHARD * j + SHARD].astype(BF)
+            slab[j, SHARD:48, :] = jnp.zeros((48 - SHARD, acc.shape[1]), BF)
+        for j in range(4):
+            @pl.when(4 * c + j != u)
+            def _():
+                sum_z(slab, zgot, ss, rs, j).start()
+
+            @pl.when(4 * c + j == u)
+            def _():
+                zgot[z] = slab[j]
+
+    def add_z(slab, zgot, ss, rs, out):
+        for zz in range(NZ):
+            @pl.when((zz != z) | (u // 4 != c))
+            def _():
+                copy(slab.at[0], zgot.at[zz], ss.at[4], rs.at[4 + zz], core_peer).wait_recv()
+        acc = zgot[0].astype(F32)
+        for zz in range(1, NZ):
+            acc += zgot[zz].astype(F32)
+        out[...] = acc[0:SHARD]
+        for j in range(4):
+            @pl.when(4 * c + j != u)
+            def _():
+                sum_z(slab, zgot, ss, rs, j).wait_send()
 
     for q in range(CHUNKS):
         w[q, mine, pl.ds(pl.multiple_of(z * MAIN, 16), MAIN), :] = w_main(q)[...]
@@ -259,7 +318,7 @@
     bias[...] = jnp.where((ki // 8) % 2 == (qi // 8) % 2, 0.0, -1e30).astype(F32)
     attend(spat, bias, probs, ft)
     mixed_all[:, lanes(s)] = ft[...].astype(BF)
-    go(gather_pair(mixed_all, mx_s, mx_r))
+    go(gather_copy(mixed_all, mx_s, mx_r, 0))
     permute(ft, fp)
     t_to_rows(fp, rows_b, D)
     bias[...] = jnp.where(ki % 8 == qi % 8, 0.0, -1e30).astype(F32)
@@ -286,35 +345,42 @@
     def spread(q):
         for k in range(1, NZ):
             z_copy(q, k).wait_recv()
-        for k in range(1, NY):
-            go(y_copy(q, k))
+        go(y_copy(q, 0))
+        go(y_copy(q, 1))
         go(c_copy(q, 0))
 
     def relay(q):
-        for k in range(1, NY):
-            y_copy(q, k).wait_recv()
-            go(c_copy(q, k))
-
-    def arrived(q):
-        for k in range(NY):
-            c_copy(q, k).wait_recv()
+        for i in range(2):
+            y_copy(q, i).wait_recv()
+            go(y_copy(q, 2 + i))
+            go(c_copy(q, 1 + i))
+
+    def complete(q):
+        for i in range(2):
+            y_copy(q, 2 + i).wait_recv()
+        go(c_copy(q, 3))
+        for i in range(4):
+            c_copy(q, i).wait_recv()
 
     def fan_out(buf, ss, rs):
-        gather_pair(buf, ss, rs).wait_recv()
-        for k in range(1, NX):
-            go(gather_x(buf, ss, rs, k, 0))
-            go(gather_x(buf, ss, rs, k, 1))
+        gather_copy(buf, ss, rs, 0).wait_recv()
+        for i in (1, 2):
+            go(gather_copy(buf, ss, rs, i))
+
+    def pass_on(buf, ss, rs):
+        for i in (1, 2):
+            gather_copy(buf, ss, rs, i).wait_recv()
+            go(gather_copy(buf, ss, rs, 2 + i))
 
     def fanned(buf, ss, rs):
-        for k in range(1, NX):
-            gather_x(buf, ss, rs, k, 0).wait_recv()
-            gather_x(buf, ss, rs, k, 1).wait_recv()
+        for i in (3, 4):
+            gather_copy(buf, ss, rs, i).wait_recv()
 
     spread(0)
     fan_out(mixed_all, mx_s, mx_r)
+    relay(0)
     spread(1)
-    relay(0)
-    arrived(0)
+    complete(0)
 
     def hidden_body(n):
         tok = regroup(tokens[:, lanes(n, 384)].astype(F32))
@@ -326,6 +392,8 @@
     hid_in[own, :] = hid[own, :]
     for k in range(1, NS):
         go(rows_copy(hid, hid_in, h_s, h_r, k))
+    pass_on(mixed_all, mx_s, mx_r)
+    relay(1)
     spread(2)
     for k in range(1, NS):
         rows_copy(hid, hid_in, h_s, h_r, k).wait_recv()
@@ -339,16 +407,13 @@
     rows_t[...] = (xh * sc[...] + sh[...]).astype(BF).astype(F32)
     rows_to_t(rows_t, ft, D)
     mod_all[:, lanes(s)] = ft[...].astype(BF)
-    go(gather_pair(mod_all, md_s, md_r))
+    go(gather_copy(mod_all, md_s, md_r, 0))
     permute(ft, fp)
     t_to_rows(fp, rows_b, D)
+    fan_out(mod_all, md_s, md_r)
     spread(3)
-    fan_out(mod_all, md_s, md_r)
 
     def project(q):
-        relay(q)
-        arrived(q)
-
         def body(n):
             acc = contract(rows_b[...], w[q, :, :, lanes(n, 384)].reshape(D, 384), 1, 0)
             acc = acc.astype(BF).astype(F32)
@@ -356,9 +421,15 @@
 
         loop(3, body)
 
+    complete(1)
     project(1)
+    relay(2)
+    complete(2)
+    pass_on(mod_all, md_s, md_r)
+    relay(3)
     project(2)
     attend(packed, bias, probs_t, None)
+    complete(3)
     project(3)
     attend_back(packed, probs_t, cot, grad)
     grad_b[...] = grad[...].astype(BF)
@@ -367,12 +438,12 @@
         go(cols_copy(grad_b, gt_all, 432, gt_s, gt_r, k))
 
     def back_body(b):
-        acc = jnp.zeros((2 * BLOCK, T), F32)
+        acc = jnp.zeros((576, T), F32)
         for q in range(1, CHUNKS):
-            acc += contract(w[q, pl.ds(2 * b, 2)].reshape(2 * BLOCK, D), grad_b[pl.ds((q - 1) * D, D), :], 1, 0)
-        fp[rows8(b * 2 * BLOCK, 2 * BLOCK), :] = acc
-
-    loop(NY, back_body)
+            acc += contract(w[q, pl.ds(NY * b, NY)].reshape(576, D), grad_b[pl.ds((q - 1) * D, D), :], 1, 0)
+        fp[rows8(b * 576, 576), :] = acc
+
+    loop(NC, back_body)
     unpermute(fp, ft)
     t_to_rows(ft, rows_t, D)
     dx = rows_t[...] * sc[...]
@@ -387,9 +458,7 @@
         rows_copy(g_out, g_in, g_s, g_r, k).wait_recv()
 
     def tok_body(j):
-        v = g_in[:, lanes(j)].astype(F32)
-        out_tok[:, lanes(j)] = ungroup(v).astype(BF)
-        gt_b[rows8(j * 128, 128), :] = v.T.astype(BF)
+        gt_b[rows8(j * 128, 128), :] = g_in[:, lanes(j)].astype(F32).T.astype(BF)
 
     loop(9, tok_body)
     g_all[:, lanes(s)] = gt_b[pl.ds(pl.multiple_of(s * 144, 16), 144), :]
@@ -397,11 +466,11 @@
         go(cols_copy(gt_b, g_all, 144, gc_s, gc_r, k))
 
     def mixed_body(b):
-        fp[rows8(b * 2 * BLOCK, 2 * BLOCK), :] = contract(
-            w[0, pl.ds(2 * b, 2)].reshape(2 * BLOCK, D), gt_b[...], 1, 0
+        fp[rows8(b * 576, 576), :] = contract(
+            w[0, pl.ds(NY * b, NY)].reshape(576, D), gt_b[...], 1, 0
         )
 
-    loop(NY, mixed_body)
+    loop(NC, mixed_body)
     unpermute(fp, ft)
 
     fanned(mod_all, md_s, md_r)
@@ -409,55 +478,37 @@
         cols_copy(grad_b, gt_all, 432, gt_s, gt_r, k).wait_recv()
 
     def gwi_body(b):
-        gwi_y[b] = contract(mod_all[rows8(b * 288, 288), :], gt_all[...], 1, 1).astype(BF)
+        gwi_p[b] = contract(mod_all[rows8(b * 288, 288), :], gt_all[...], 1, 1).astype(BF)
 
     loop(NY, gwi_body)
-    for k in range(1, NY):
-        go(sum_y(gwi_y, gwi_yin, ri_s, ri_r, k))
-
+    go(sum_c(gwi_p, gwi_c, ri_s, ri_r))
     fanned(mixed_all, mx_s, mx_r)
     for k in range(1, NS):
         cols_copy(gt_b, g_all, 144, gc_s, gc_r, k).wait_recv()
 
     def gwo_body(b):
-        gwo_y[b] = contract(mixed_all[rows8(b * 288, 288), :], g_all[...], 1, 1).astype(BF)
+        gwo_p[b] = contract(mixed_all[rows8(b * 288, 288), :], g_all[...], 1, 1).astype(BF)
 
     loop(NY, gwo_body)
-    for k in range(1, NY):
-        go(sum_y(gwo_y, gwo_yin, ro_s, ro_r, k))
-
-    def add_y(src, dst, ss, rs, out):
-        for k in range(1, NY):
-            sum_y(src, dst, ss, rs, k).wait_recv()
-        acc = src[y].astype(F32)
-        for k in range(1, NY):
-            acc += dst[k - 1].astype(F32)
-        for i in range(8):
-            out[i, 0:SHARD, :] = acc[SHARD * i : SHARD * i + SHARD].astype(BF)
-            out[i, SHARD:48, :] = jnp.zeros((48 - SHARD, acc.shape[1]), BF)
-
-    def add_z(src, dst, ss, rs, out):
-        for k in range(1, 8):
-            sum_z(src, dst, ss, rs, k).wait_recv()
-        acc = src[u].astype(F32)
-        for k in range(1, 8):
-            acc += dst[k - 1].astype(F32)
-        out[...] = acc[0:SHARD]
-
-    attend_back(spat, probs, ft, grad)
-    add_y(gwi_y, gwi_yin, ri_s, ri_r, gwi_z)
-    for k in range(1, 8):
-        go(sum_z(gwi_z, gwi_zin, si_s, si_r, k))
-    add_y(gwo_y, gwo_yin, ro_s, ro_r, gwo_z)
-    for k in range(1, 8):
-        go(sum_z(gwo_z, gwo_zin, so_s, so_r, k))
+    go(sum_c(gwo_p, gwo_c, ro_s, ro_r))
+    add_c(gwi_p, gwi_c, gwi_h, gwi_y, ri_s, ri_r)
+    add_c(gwo_p, gwo_c, gwo_h, gwo_y, ro_s, ro_r)
 
     def out_body(j):
+        out_tok[:, lanes(j)] = ungroup(g_in[:, lanes(j)].astype(F32)).astype(BF)
+
+    loop(9, out_body)
+    attend_back(spat, probs, ft, grad, 0, 12)
+    add_y(gwi_h, gwi_y, gwi_t, gwi_z, ri_s, ri_r)
+    add_y(gwo_h, gwo_y, gwo_t, gwo_z, ro_s, ro_r)
+    attend_back(spat, probs, ft, grad, 12, 4)
+
+    def qkv_body(j):
         out_qkv[:, lanes(j)] = ungroup(grad[rows8(j * 128, 128), :].T).astype(BF)
 
-    loop(27, out_body)
-    add_z(gwi_z, gwi_zin, si_s, si_r, out_gwi)
-    add_z(gwo_z, gwo_zin, so_s, so_r, out_gwo)
+    loop(27, qkv_body)
+    add_z(gwi_t, gwi_z, ri_s, ri_r, out_gwi)
+    add_z(gwo_t, gwo_z, ro_s, ro_r, out_gwo)
     for cp in started:
         cp.wait_send()
 
@@ -504,18 +555,12 @@
         VMEM((D, T), F32),
         VMEM((T, D), BF),
         VMEM((D, T), BF),
-        VMEM((NY, 288, 432), BF),
-        VMEM((NY, 288, 144), BF),
-        VMEM((3, 288, 432), BF),
-        VMEM((3, 288, 144), BF),
-        VMEM((8, 48, 432), BF),
-        VMEM((8, 48, 144), BF),
-        VMEM((7, 48, 432), BF),
-        VMEM((7, 48, 144), BF),
-        dma(4, 3), dma(4, 3), dma(3), dma(3), dma(4, 3), dma(4, 3), dma(4, 4), dma(4, 4),
-        dma(7), dma(7), dma(7), dma(7),
+        *[VMEM(n + (m,), BF) for m in (432, 144)
+          for n in ((NY, 288), (NY, 144), (NY, 144), (3, 144), (4, 48), (4, 48))],
+        dma(4, 3), dma(4, 3), dma(3), dma(3), dma(4, 4), dma(4, 4), dma(4, 4), dma(4, 4),
+        dma(5), dma(5), dma(5), dma(5),
         dma(7), dma(7), dma(7), dma(7), dma(7), dma(7), dma(7), dma(7),
-        dma(3), dma(3), dma(3), dma(3), dma(7), dma(7), dma(7), dma(7),
+        dma(8), dma(8), dma(8), dma(8),
     ]
     spec = pl.BlockSpec(memory_space=VMEM)
     gq, gt, gwo, gwi = pl.pallas_call(

time: 171 us -> 153 us (0.89)
  Pallas kernels: 163 us -> 145 us
    pallas_call x1, Pallas kernels: 163 us -> 145 us  [shards(): pl.pallas_call(kernel, out_shape=(jax.ShapeDtypeStruct((T, 3 * D), BF), j...]
where the time goes in v2:
time: 153 us
  Pallas kernels  145 us (95%)
  local copies, waits for them, and re-layouts  5.91 us (4%)
    pallas_call x1, Pallas kernels, shards(): pl.pallas_call(kernel, out_shape=(jax.ShapeDtypeStruct((T, 3 * D), BF), j...  145 us
    unnamed x10, local copies, waits for them, and re-layouts  4.5 us

profile of v2, /device:TPU:1, one launch (start us, length us, event | category | flops | bytes accessed | tf_op | source)
XLA Modules:
  0.0 152.7 jit_solution(13044811331034048865)
XLA Ops:
  1.4 0.7 maximum_multiply_fusion.1
  2.0 0.0 slice-start
  2.0 0.0 slice-start.1
  2.0 0.7 slice-done
  2.8 0.0 slice-done.1
  2.8 0.6 copy.11
  3.5 144.7 %shard_map.93 = (bf16[128,3456]{1,0:T(8,128)(2,1)}, bf16[128,1152]{1,0:T(8,128)(2,1)}, f32[36,144]{1,0:T(8,128)}, f32[36,432]{1,0:T(8,128)}) custom-call(bf16[128,3456]{1,0:T(8,128)(2,1)} %bitcast.8, bf16[128,1152]{1,0:T(8,128)(2,1)} %bitcast.10, bf16[128,1152]{1,0:T(8,128)(2,1)} %bitcast.11, bf16[36,1152]{1,0:T(8,128)(2,1)} %wo.1, bf16[36,3456]{1,0:T(8,128)(2,1)} %wi.1, ...), custom_call_target="tpu_custom_call" | custom-call | tf_op jit(solution)/shard_map/pallas_call | solution.py:566
  148.2 0.0 copy-start
  148.2 2.2 %copy.17 = bf16[1,2,64,3456]{3,2,1,0:T(8,128)(2,1)} copy(bf16[1,2,64,3456]{3,2,1,0:T(8,128)(2,1)} %bitcast.9) | data formatting | bytes 1769472
  150.4 0.0 copy-done
  150.4 0.0 copy-start.2
  150.4 0.7 copy.18
  151.1 0.1 copy-done.2
  151.2 0.0 copy-start.1
  151.2 0.6 copy.19
  151.8 0.3 copy-done.1
  152.1 0.6 copy.20
  (5 shorter events, 0.1 us)
Async XLA Ops:
  2.0 0.7 slice-start
  2.0 0.7 slice-start.1
  148.2 2.2 %copy-start = (bf16[128,1152]{1,0:T(8,128)(2,1)S(1)}, bf16[128,1152]{1,0:T(8,128)(2,1)}, u32[]{:S(2)}) copy-start(bf16[128,1152]{1,0:T(8,128)(2,1)} %get-tuple-element.9) | copy-start | bytes 884740
  150.4 0.8 copy-start.2
  151.2 0.9 copy-start.1

commit v3 on v2

--- a/solution.py
+++ b/solution.py
@@ -17,7 +17,10 @@
 SHARD = 36
 MAIN, TAIL = 32, 4
 BLOCK = NZ * SHARD
-CHUNKS = 4
+UNIT = 384
+FIRST = (0, 3, 10, 6)
+COUNT = (3, 3, 2, 4)
+SHARED = 3
 F32, BF = jnp.float32, jnp.bfloat16
 MESH = pl.DeviceIdType.MESH
 SCALE = 1.0 / math.sqrt(HEAD)
@@ -141,7 +144,7 @@
     w, tails, packed, spat, probs, probs_t, bias, grad, grad_b, ft, fp, rows_b, rows_t, hid, hid_in, g_out,
     xhat, rstd, mixed_all, mod_all, gt_all, g_all, cot, g_in, gt_b,
     gwi_p, gwi_c, gwi_h, gwi_y, gwi_t, gwi_z, gwo_p, gwo_c, gwo_h, gwo_y, gwo_t, gwo_z,
-    z_s, z_r, t_s, t_r, y_s, y_r, c_s, c_r, mx_s, mx_r, md_s, md_r,
+    z_s, z_r, t_s, t_r, y_s, y_r, x_s, x_r, c_s, c_r, mx_s, mx_r, md_s, md_r,
     h_s, h_r, g_s, g_r, gt_s, gt_r, gc_s, gc_r, ri_s, ri_r, ro_s, ro_r,
 ):
     d = lax.axis_index("dp")
@@ -149,7 +152,6 @@
     y, u = d // 8, d % 8
     z, c = u // 2, u % 2
     x, zl = s // 2, s % 2
-    mine = c * NY + y
 
     def z_peer(k):
         return (y * 8 + lax.rem(z + k, NZ) * 2 + c, s)
@@ -192,33 +194,44 @@
         cp.start()
         started.append(cp)
 
-    def w_main(q):
-        if q == 0:
-            return wo.at[pl.ds(0, MAIN), :]
-        return wi.at[pl.ds(0, MAIN), pl.ds((q - 1) * D, D)]
+    def units(q):
+        if q == SHARED:
+            return pl.ds(FIRST[q] + x, 1)
+        return pl.ds(FIRST[q], COUNT[q])
+
+    main_rows = pl.ds(pl.multiple_of(z * MAIN, 16), MAIN)
 
     def z_copy(q, k):
-        return copy(
-            w_main(q), w.at[q, mine, pl.ds(pl.multiple_of(z * MAIN, 16), MAIN), :],
-            z_s.at[q, k - 1], z_r.at[q, k - 1], z_peer(k),
-        )
+        part = w.at[units(q), c, y, main_rows, :]
+        return copy(part, part, z_s.at[q, k - 1], z_r.at[q, k - 1], z_peer(k))
 
     def t_copy(k):
         return copy(tail, tails.at[z], t_s.at[k - 1], t_r.at[k - 1], z_peer(k))
 
-    def block(k):
-        return c * NY + lax.rem(y + NY + k, NY)
+    def at_y(k):
+        return lax.rem(y + NY + k, NY)
+
+    def at_x(k):
+        return FIRST[SHARED] + lax.rem(x + NX + k, NX)
 
     def y_copy(q, i):
-        part = w.at[q, mine]
+        part = w.at[units(q), c, y]
         if i == 2:
-            part = w.at[q, block(-1), pl.ds(0, 80), :]
+            part = w.at[units(q), c, at_y(-1), pl.ds(0, 80), :]
         if i == 3:
-            part = w.at[q, block(1), pl.ds(80, 64), :]
+            part = w.at[units(q), c, at_y(1), pl.ds(80, 64), :]
         return copy(part, part, y_s.at[q, i], y_r.at[q, i], y_peer(1 if i % 2 == 0 else 3))
 
+    def x_copy(i):
+        if i < 2:
+            part = w.at[at_x(0), c]
+        else:
+            part = w.at[at_x(-1 if i == 2 else 1), c, pl.ds(2 * (i - 2), 2)]
+        return copy(part, part, x_s.at[i], x_r.at[i], x_peer(1 if i % 2 == 0 else 3))
+
     def c_copy(q, i):
-        part = w.at[q, block((0, -1, 1, 2)[i])]
+        step = (0, -1, 1, 2)[i]
+        part = w.at[at_x(step), c] if q == SHARED else w.at[units(q), c, at_y(step)]
         return copy(part, part, c_s.at[q, i], c_r.at[q, i], core_peer)
 
     def gather_copy(buf, ss, rs, i):
@@ -301,64 +314,87 @@
             def _():
                 sum_z(slab, zgot, ss, rs, j).wait_send()
 
-    for q in range(CHUNKS):
-        w[q, mine, pl.ds(pl.multiple_of(z * MAIN, 16), MAIN), :] = w_main(q)[...]
+    for n in range(3):
+        w[n, c, y, main_rows, :] = wo[0:MAIN, n * UNIT : n * UNIT + UNIT]
+    for n in (3, 4, 5, 10, 11):
+        w[n, c, y, main_rows, :] = wi[0:MAIN, (n - 3) * UNIT : (n - 2) * UNIT]
+    w[at_x(0), c, y, main_rows, :] = wi[0:MAIN, lanes(at_x(0) - 3, UNIT)]
     tails[z] = tail[...]
     pl.semaphore_wait(barrier, len(peers))
 
     for k in range(1, NZ):
         go(t_copy(k))
-    for q in range(CHUNKS):
+    for q in (SHARED, 0, 1, 2):
         for k in range(1, NZ):
             go(z_copy(q, k))
 
     rows_to_t(qkv, spat, 3 * D, group=True)
-    ki = lax.broadcasted_iota(jnp.int32, (T, T), 0)
-    qi = lax.broadcasted_iota(jnp.int32, (T, T), 1)
-    bias[...] = jnp.where((ki // 8) % 2 == (qi // 8) % 2, 0.0, -1e30).astype(F32)
-    attend(spat, bias, probs, ft)
-    mixed_all[:, lanes(s)] = ft[...].astype(BF)
-    go(gather_copy(mixed_all, mx_s, mx_r, 0))
-    permute(ft, fp)
-    t_to_rows(fp, rows_b, D)
-    bias[...] = jnp.where(ki % 8 == qi % 8, 0.0, -1e30).astype(F32)
-    rows_to_t(gout, cot, D)
 
     for k in range(1, NZ):
         t_copy(k).wait_recv()
 
     low = lax.broadcasted_iota(jnp.int32, (8, 128), 0) < 4
 
-    def tail_body(m):
+    def tail_tiles(m):
         full = [tails[zz, pl.ds(pl.multiple_of(m * 16, 16), 16), :].astype(F32) for zz in range(NZ)]
+        tiles = []
         for half in range(2):
             a = [v[8 * half : 8 * half + 8] for v in full]
             r = [pltpu.roll(v, 4, 0) for v in a]
             even = [jnp.where(low, a[0], r[1]), jnp.where(low, a[2], r[3])]
             odd = [jnp.where(low, r[0], a[1]), jnp.where(low, r[2], a[3])]
-            for i, pieces in enumerate((even, odd)):
-                j = 4 * m + 2 * half + i
-                w[j // 9, mine, pl.ds(NZ * MAIN, 16), lanes(j % 9)] = jnp.concatenate(pieces, axis=0).astype(BF)
-
-    loop(9, tail_body)
+            tiles += [jnp.concatenate(t, axis=0).astype(BF) for t in (even, odd)]
+        return tiles
+
+    for m in range(9):
+        for i, tile in enumerate(tail_tiles(m)):
+            n, j = divmod(4 * m + i, 3)
+
+            def put():
+                w[n, c, y, pl.ds(NZ * MAIN, 16), pl.ds(128 * j, 128)] = tile
+
+            if FIRST[SHARED] <= n < FIRST[SHARED] + NX:
+                pl.when(x == n - FIRST[SHARED])(put)
+            else:
+                put()
 
     def spread(q):
         for k in range(1, NZ):
             z_copy(q, k).wait_recv()
         go(y_copy(q, 0))
         go(y_copy(q, 1))
-        go(c_copy(q, 0))
+        if q != SHARED:
+            go(c_copy(q, 0))
 
     def relay(q):
         for i in range(2):
             y_copy(q, i).wait_recv()
             go(y_copy(q, 2 + i))
-            go(c_copy(q, 1 + i))
+            if q != SHARED:
+                go(c_copy(q, 1 + i))
 
     def complete(q):
         for i in range(2):
             y_copy(q, 2 + i).wait_recv()
-        go(c_copy(q, 3))
+        if q == SHARED:
+            go(x_copy(0))
+            go(x_copy(1))
+            go(c_copy(q, 0))
+        else:
+            go(c_copy(q, 3))
+
+    def x_relay():
+        for i in range(2):
+            x_copy(i).wait_recv()
+            go(x_copy(2 + i))
+            go(c_copy(SHARED, 1 + i))
+
+    def x_complete():
+        for i in range(2):
+            x_copy(2 + i).wait_recv()
+        go(c_copy(SHARED, 3))
+
+    def both_cores(q):
         for i in range(4):
             c_copy(q, i).wait_recv()
 
@@ -376,15 +412,34 @@
         for i in (3, 4):
             gather_copy(buf, ss, rs, i).wait_recv()
 
+    def weight(n):
+        return w[n].reshape(D, UNIT)
+
+    spread(SHARED)
+
+    ki = lax.broadcasted_iota(jnp.int32, (T, T), 0)
+    qi = lax.broadcasted_iota(jnp.int32, (T, T), 1)
+    bias[...] = jnp.where((ki // 8) % 2 == (qi // 8) % 2, 0.0, -1e30).astype(F32)
+    attend(spat, bias, probs, ft)
     spread(0)
-    fan_out(mixed_all, mx_s, mx_r)
+    relay(SHARED)
+    mixed_all[:, lanes(s)] = ft[...].astype(BF)
+    permute(ft, fp)
+    t_to_rows(fp, rows_b, D)
+    complete(SHARED)
+    bias[...] = jnp.where(ki % 8 == qi % 8, 0.0, -1e30).astype(F32)
+    rows_to_t(gout, cot, D)
+    spread(1)
     relay(0)
-    spread(1)
+    spread(2)
+    x_relay()
     complete(0)
+    go(gather_copy(mixed_all, mx_s, mx_r, 0))
+    both_cores(0)
 
     def hidden_body(n):
         tok = regroup(tokens[:, lanes(n, 384)].astype(F32))
-        acc = contract(rows_b[...], w[0, :, :, lanes(n, 384)].reshape(D, 384), 1, 0)
+        acc = contract(rows_b[...], weight(n), 1, 0)
         hid[:, lanes(n, 384)] = (tok + acc).astype(BF)
 
     loop(3, hidden_body)
@@ -392,11 +447,11 @@
     hid_in[own, :] = hid[own, :]
     for k in range(1, NS):
         go(rows_copy(hid, hid_in, h_s, h_r, k))
-    pass_on(mixed_all, mx_s, mx_r)
     relay(1)
-    spread(2)
+    x_complete()
     for k in range(1, NS):
         rows_copy(hid, hid_in, h_s, h_r, k).wait_recv()
+    fan_out(mixed_all, mx_s, mx_r)
 
     hf = hid_in[...].astype(F32)
     centred = hf - jnp.mean(hf, axis=-1, keepdims=True)
@@ -410,37 +465,37 @@
     go(gather_copy(mod_all, md_s, md_r, 0))
     permute(ft, fp)
     t_to_rows(fp, rows_b, D)
+    complete(1)
+    relay(2)
     fan_out(mod_all, md_s, md_r)
-    spread(3)
-
-    def project(q):
-        def body(n):
-            acc = contract(rows_b[...], w[q, :, :, lanes(n, 384)].reshape(D, 384), 1, 0)
-            acc = acc.astype(BF).astype(F32)
-            packed[rows8((q - 1) * D + n * 384, 384), :] = acc.T
-
-        loop(3, body)
-
-    complete(1)
-    project(1)
-    relay(2)
+
+    def project(first, count):
+        def body(i):
+            acc = contract(rows_b[...], weight(first + i), 1, 0)
+            packed[rows8((first - 3 + i) * UNIT, UNIT), :] = acc.astype(BF).astype(F32).T
+
+        loop(count, body)
+
+    both_cores(SHARED)
+    project(6, 4)
+    both_cores(1)
+    project(3, 3)
+    pass_on(mixed_all, mx_s, mx_r)
     complete(2)
-    pass_on(mod_all, md_s, md_r)
-    relay(3)
-    project(2)
     attend(packed, bias, probs_t, None)
-    complete(3)
-    project(3)
+    both_cores(2)
+    project(10, 2)
     attend_back(packed, probs_t, cot, grad)
     grad_b[...] = grad[...].astype(BF)
     gt_all[:, lanes(s)] = grad_b[pl.ds(pl.multiple_of(s * 432, 16), 432), :]
-    for k in range(1, NS):
-        go(cols_copy(grad_b, gt_all, 432, gt_s, gt_r, k))
+
+    def weight_t(n, b):
+        return jnp.concatenate([w[n + i, b].reshape(576, UNIT) for i in range(3)], axis=1)
 
     def back_body(b):
         acc = jnp.zeros((576, T), F32)
-        for q in range(1, CHUNKS):
-            acc += contract(w[q, pl.ds(NY * b, NY)].reshape(576, D), grad_b[pl.ds((q - 1) * D, D), :], 1, 0)
+        for q in range(3):
+            acc += contract(weight_t(3 + 3 * q, b), grad_b[pl.ds(q * D, D), :], 1, 0)
         fp[rows8(b * 576, 576), :] = acc
 
     loop(NC, back_body)
@@ -455,6 +510,9 @@
     for k in range(1, NS):
         go(rows_copy(g_out, g_in, g_s, g_r, k))
     for k in range(1, NS):
+        go(cols_copy(grad_b, gt_all, 432, gt_s, gt_r, k))
+    pass_on(mod_all, md_s, md_r)
+    for k in range(1, NS):
         rows_copy(g_out, g_in, g_s, g_r, k).wait_recv()
 
     def tok_body(j):
@@ -467,11 +525,18 @@
 
     def mixed_body(b):
         fp[rows8(b * 576, 576), :] = contract(
-            w[0, pl.ds(NY * b, NY)].reshape(576, D), gt_b[...], 1, 0
+            weight_t(0, b), gt_b[...], 1, 0
         )
 
     loop(NC, mixed_body)
     unpermute(fp, ft)
+
+    attend_back(spat, probs, ft, grad)
+
+    def out_body(j):
+        out_tok[:, lanes(j)] = ungroup(g_in[:, lanes(j)].astype(F32)).astype(BF)
+
+    loop(9, out_body)
 
     fanned(mod_all, md_s, md_r)
     for k in range(1, NS):
@@ -494,19 +559,12 @@
     add_c(gwi_p, gwi_c, gwi_h, gwi_y, ri_s, ri_r)
     add_c(gwo_p, gwo_c, gwo_h, gwo_y, ro_s, ro_r)
 
-    def out_body(j):
-        out_tok[:, lanes(j)] = ungroup(g_in[:, lanes(j)].astype(F32)).astype(BF)
-
-    loop(9, out_body)
-    attend_back(spat, probs, ft, grad, 0, 12)
+    def qkv_body(j):
+        out_qkv[:, lanes(j)] = ungroup(grad[rows8(j * 128, 128), :].T).astype(BF)
+
+    loop(27, qkv_body)
     add_y(gwi_h, gwi_y, gwi_t, gwi_z, ri_s, ri_r)
     add_y(gwo_h, gwo_y, gwo_t, gwo_z, ro_s, ro_r)
-    attend_back(spat, probs, ft, grad, 12, 4)
-
-    def qkv_body(j):
-        out_qkv[:, lanes(j)] = ungroup(grad[rows8(j * 128, 128), :].T).astype(BF)
-
-    loop(27, qkv_body)
     add_z(gwi_t, gwi_z, ri_s, ri_r, out_gwi)
     add_z(gwo_t, gwo_z, ro_s, ro_r, out_gwo)
     for cp in started:
@@ -530,7 +588,7 @@
     tail = tail.reshape(TAIL, 36, 128).transpose(1, 0, 2).reshape(144, 128)
     dma = lambda *n: DMA(n)
     scratch = [
-        VMEM((CHUNKS, NY * NC, BLOCK, D), BF),
+        VMEM((12, NC, NY, BLOCK, UNIT), BF),
         VMEM((NZ, 144, 128), BF),
         VMEM((3 * D, T), F32),
         VMEM((3 * D, T), F32),
@@ -557,7 +615,7 @@
         VMEM((D, T), BF),
         *[VMEM(n + (m,), BF) for m in (432, 144)
           for n in ((NY, 288), (NY, 144), (NY, 144), (3, 144), (4, 48), (4, 48))],
-        dma(4, 3), dma(4, 3), dma(3), dma(3), dma(4, 4), dma(4, 4), dma(4, 4), dma(4, 4),
+        dma(4, 3), dma(4, 3), dma(3), dma(3), dma(4, 4), dma(4, 4), dma(4), dma(4), dma(4, 4), dma(4, 4),
         dma(5), dma(5), dma(5), dma(5),
         dma(7), dma(7), dma(7), dma(7), dma(7), dma(7), dma(7), dma(7),
         dma(8), dma(8), dma(8), dma(8),

time: 153 us -> 149 us (0.974)
  Pallas kernels: 145 us -> 141 us
    pallas_call x1, Pallas kernels: 145 us -> 141 us  [shards(): pl.pallas_call(kernel, out_shape=(jax.ShapeDtypeStruct((T, 3 * D), BF), j...]
where the time goes in v3:
time: 149 us
  Pallas kernels  141 us (95%)
  local copies, waits for them, and re-layouts  5.91 us (4%)
    pallas_call x1, Pallas kernels, shards(): pl.pallas_call(kernel, out_shape=(jax.ShapeDtypeStruct((T, 3 * D), BF), j...  141 us
    unnamed x10, local copies, waits for them, and re-layouts  4.5 us

profile of v3, /device:TPU:1, one launch (start us, length us, event | category | flops | bytes accessed | tf_op | source)
XLA Modules:
  0.0 149.0 jit_solution(16753612968565028309)
XLA Ops:
  1.4 0.7 maximum_multiply_fusion.1
  2.0 0.0 slice-start
  2.0 0.0 slice-start.1
  2.0 0.7 slice-done
  2.8 0.0 slice-done.1
  2.8 0.6 copy.11
  3.5 141.0 %shard_map.93 = (bf16[128,3456]{1,0:T(8,128)(2,1)}, bf16[128,1152]{1,0:T(8,128)(2,1)}, f32[36,144]{1,0:T(8,128)}, f32[36,432]{1,0:T(8,128)}) custom-call(bf16[128,3456]{1,0:T(8,128)(2,1)} %bitcast.8, bf16[128,1152]{1,0:T(8,128)(2,1)} %bitcast.10, bf16[128,1152]{1,0:T(8,128)(2,1)} %bitcast.11, bf16[36,1152]{1,0:T(8,128)(2,1)} %wo.1, bf16[36,3456]{1,0:T(8,128)(2,1)} %wi.1, ...), custom_call_target="tpu_custom_call" | custom-call | tf_op jit(solution)/shard_map/pallas_call | solution.py:624
  144.4 0.0 copy-start
  144.5 2.2 %copy.17 = bf16[1,2,64,3456]{3,2,1,0:T(8,128)(2,1)} copy(bf16[1,2,64,3456]{3,2,1,0:T(8,128)(2,1)} %bitcast.9) | data formatting | bytes 1769472
  146.6 0.0 copy-done
  146.6 0.0 copy-start.2
  146.6 0.7 copy.18
  147.4 0.1 copy-done.2
  147.4 0.0 copy-start.1
  147.4 0.6 copy.19
  148.0 0.3 copy-done.1
  148.3 0.6 copy.20
  (5 shorter events, 0.1 us)
Async XLA Ops:
  2.0 0.7 slice-start
  2.0 0.7 slice-start.1
  144.4 2.2 %copy-start = (bf16[128,1152]{1,0:T(8,128)(2,1)S(1)}, bf16[128,1152]{1,0:T(8,128)(2,1)}, u32[]{:S(2)}) copy-start(bf16[128,1152]{1,0:T(8,128)(2,1)} %get-tuple-element.9) | copy-start | bytes 884740
  146.6 0.8 copy-start.2
  147.4 0.9 copy-start.1

commit v4 on v3

--- a/solution.py
+++ b/solution.py
@@ -11,16 +11,18 @@
 HEADS = 16
 D = 1152
 HEAD = D // HEADS
+GROUP = 4
 T = 128
 NY, NZ, NC, NS = 4, 4, 2, 8
 NX = 4
 SHARD = 36
 MAIN, TAIL = 32, 4
 BLOCK = NZ * SHARD
-UNIT = 384
-FIRST = (0, 3, 10, 6)
-COUNT = (3, 3, 2, 4)
+TILE = 128
+FIRST = (0, 17, 27, 9)
+COUNT = (9, 10, 9, 8)
 SHARED = 3
+PER_X = 2
 F32, BF = jnp.float32, jnp.bfloat16
 MESH = pl.DeviceIdType.MESH
 SCALE = 1.0 / math.sqrt(HEAD)
@@ -103,7 +105,7 @@
 
 def attend(packed, bias, probs, out):
     def body(h):
-        for hh in (2 * h, 2 * h + 1):
+        for hh in [GROUP * h + i for i in range(GROUP)]:
             q = packed[rows8(HEAD * hh, HEAD), :].astype(BF)
             k = packed[rows8(D + HEAD * hh, HEAD), :].astype(BF)
             s = contract(k, q, 0, 0) * SCALE + bias[...]
@@ -115,13 +117,13 @@
                 o = contract(v, p.astype(BF), 1, 0)
                 out[rows8(HEAD * hh, HEAD), :] = o.astype(BF).astype(F32)
 
-    loop(HEADS // 2, body)
+    loop(HEADS // GROUP, body)
 
 
 def attend_back(packed, probs, cot, grad, first=0, count=HEADS):
     def body(h):
-        h = h + first // 2
-        for hh in (2 * h, 2 * h + 1):
+        h = h + first // GROUP
+        for hh in [GROUP * h + i for i in range(GROUP)]:
             q, k, v = head_slices(packed, hh)
             do = cot[rows8(HEAD * hh, HEAD), :].astype(BF)
             p = probs[hh]
@@ -135,16 +137,16 @@
             grad[rows8(D + HEAD * hh, HEAD), :] = dk
             grad[rows8(2 * D + HEAD * hh, HEAD), :] = dv
 
-    loop(count // 2, body)
+    loop(count // GROUP, body)
 
 
 def kernel(
-    qkv, tokens, gout, wo, wi, tail, sc, sh,
+    qkv_h, tokens_h, gout_h, wo_h, wi_h, sc, sh,
     out_qkv, out_tok, out_gwo, out_gwi,
-    w, tails, packed, spat, probs, probs_t, bias, grad, grad_b, ft, fp, rows_b, rows_t, hid, hid_in, g_out,
+    qkv, tokens, gout, wo, wi, tail, w, tails, packed, spat, probs, probs_t, bias, grad, grad_b, ft, fp, rows_b, rows_t, hid, hid_in, g_out,
     xhat, rstd, mixed_all, mod_all, gt_all, g_all, cot, g_in, gt_b,
     gwi_p, gwi_c, gwi_h, gwi_y, gwi_t, gwi_z, gwo_p, gwo_c, gwo_h, gwo_y, gwo_t, gwo_z,
-    z_s, z_r, t_s, t_r, y_s, y_r, x_s, x_r, c_s, c_r, mx_s, mx_r, md_s, md_r,
+    in_s, z_s, z_r, t_s, t_r, y_s, y_r, x_s, x_r, c_s, c_r, mx_s, mx_r, md_s, md_r,
     h_s, h_r, g_s, g_r, gt_s, gt_r, gc_s, gc_r, ri_s, ri_r, ro_s, ro_r,
 ):
     d = lax.axis_index("dp")
@@ -179,6 +181,14 @@
         + [s_peer(k) for k in range(1, NS)]
     )
     peers = peers[3:]
+    loads = [
+        pltpu.make_async_copy(a, b, in_s.at[i])
+        for i, (a, b) in enumerate(
+            ((wi_h, wi), (wo_h, wo), (qkv_h, qkv), (gout_h, gout), (tokens_h, tokens))
+        )
+    ]
+    for cp in loads:
+        cp.start()
     barrier = pltpu.get_barrier_semaphore()
     for p in peers:
         pl.semaphore_signal(barrier, inc=1, device_id=p, device_id_type=MESH)
@@ -194,9 +204,12 @@
         cp.start()
         started.append(cp)
 
+    def at_x(k):
+        return FIRST[SHARED] + PER_X * lax.rem(x + NX + k, NX)
+
     def units(q):
         if q == SHARED:
-            return pl.ds(FIRST[q] + x, 1)
+            return pl.ds(at_x(0), PER_X)
         return pl.ds(FIRST[q], COUNT[q])
 
     main_rows = pl.ds(pl.multiple_of(z * MAIN, 16), MAIN)
@@ -210,9 +223,6 @@
 
     def at_y(k):
         return lax.rem(y + NY + k, NY)
-
-    def at_x(k):
-        return FIRST[SHARED] + lax.rem(x + NX + k, NX)
 
     def y_copy(q, i):
         part = w.at[units(q), c, y]
@@ -224,25 +234,22 @@
 
     def x_copy(i):
         if i < 2:
-            part = w.at[at_x(0), c]
+            part = w.at[units(SHARED), c]
         else:
-            part = w.at[at_x(-1 if i == 2 else 1), c, pl.ds(2 * (i - 2), 2)]
+            part = w.at[pl.ds(at_x(-1 if i == 2 else 1), PER_X), c, pl.ds(2 * (i - 2), 2)]
         return copy(part, part, x_s.at[i], x_r.at[i], x_peer(1 if i % 2 == 0 else 3))
 
     def c_copy(q, i):
         step = (0, -1, 1, 2)[i]
-        part = w.at[at_x(step), c] if q == SHARED else w.at[units(q), c, at_y(step)]
+        part = w.at[pl.ds(at_x(step), PER_X), c] if q == SHARED else w.at[units(q), c, at_y(step)]
         return copy(part, part, c_s.at[q, i], c_r.at[q, i], core_peer)
 
+    other = s + 1 - 2 * zl
+
     def gather_copy(buf, ss, rs, i):
-        if i == 0:
-            part, to = buf.at[:, lanes(s)], pair
-        elif i < 3:
-            part, to = buf.at[:, lanes(x, 256)], x_peer(1 if i == 1 else 3)
-        elif i == 3:
-            part, to = buf.at[:, lanes(2 * lax.rem(x + 3, NX))], x_peer(1)
-        else:
-            part, to = buf.at[:, lanes(2 * lax.rem(x + 1, NX) + 1)], x_peer(3)
+        slot = (s, s, s, other, other, 2 * lax.rem(x + 3, NX) + zl, 2 * lax.rem(x + 1, NX) + 1 - zl)[i]
+        to = pair if i == 0 else x_peer(1 if i % 2 == 1 else 3)
+        part = buf.at[:, lanes(slot)]
         return copy(part, part, ss.at[i], rs.at[i], to)
 
     def rows_copy(src, dst, ss, rs, k):
@@ -314,21 +321,33 @@
             def _():
                 sum_z(slab, zgot, ss, rs, j).wait_send()
 
-    for n in range(3):
-        w[n, c, y, main_rows, :] = wo[0:MAIN, n * UNIT : n * UNIT + UNIT]
-    for n in (3, 4, 5, 10, 11):
-        w[n, c, y, main_rows, :] = wi[0:MAIN, (n - 3) * UNIT : (n - 2) * UNIT]
-    w[at_x(0), c, y, main_rows, :] = wi[0:MAIN, lanes(at_x(0) - 3, UNIT)]
+    for cp in loads[:2]:
+        cp.wait()
+    pieces = []
+    for ref in (wo, wi):
+        rows = ref[MAIN:SHARD, :].astype(F32)
+        pieces += [rows[:, j * TILE : j * TILE + TILE] for j in range(rows.shape[1] // TILE)]
+    tail[...] = jnp.concatenate(pieces, axis=0).astype(BF)
+    for n in range(9):
+        w[n, c, y, main_rows, :] = wo[0:MAIN, n * TILE : n * TILE + TILE]
+    for n in range(17, 36):
+        w[n, c, y, main_rows, :] = wi[0:MAIN, (n - 9) * TILE : (n - 8) * TILE]
+    for i in range(PER_X):
+        w[at_x(0) + i, c, y, main_rows, :] = wi[0:MAIN, lanes(at_x(0) + i - 9)]
     tails[z] = tail[...]
+    loads[2].wait()
+    rows_to_t(qkv, spat, 3 * D, group=True)
     pl.semaphore_wait(barrier, len(peers))
 
     for k in range(1, NZ):
         go(t_copy(k))
-    for q in (SHARED, 0, 1, 2):
+
+    def z_start(q):
         for k in range(1, NZ):
             go(z_copy(q, k))
 
-    rows_to_t(qkv, spat, 3 * D, group=True)
+    z_start(SHARED)
+    z_start(0)
 
     for k in range(1, NZ):
         t_copy(k).wait_recv()
@@ -348,13 +367,13 @@
 
     for m in range(9):
         for i, tile in enumerate(tail_tiles(m)):
-            n, j = divmod(4 * m + i, 3)
-
-            def put():
-                w[n, c, y, pl.ds(NZ * MAIN, 16), pl.ds(128 * j, 128)] = tile
-
-            if FIRST[SHARED] <= n < FIRST[SHARED] + NX:
-                pl.when(x == n - FIRST[SHARED])(put)
+            n = 4 * m + i
+
+            def put(n=n, tile=tile):
+                w[n, c, y, pl.ds(NZ * MAIN, 16), :] = tile
+
+            if FIRST[SHARED] <= n < FIRST[SHARED] + COUNT[SHARED]:
+                pl.when(x == (n - FIRST[SHARED]) // PER_X)(put)
             else:
                 put()
 
@@ -398,22 +417,29 @@
         for i in range(4):
             c_copy(q, i).wait_recv()
 
-    def fan_out(buf, ss, rs):
+    def fan_own(buf, ss, rs):
+        for i in (0, 1, 2):
+            go(gather_copy(buf, ss, rs, i))
+
+    def fan_other(buf, ss, rs):
         gather_copy(buf, ss, rs, 0).wait_recv()
-        for i in (1, 2):
+        for i in (3, 4):
             go(gather_copy(buf, ss, rs, i))
 
-    def pass_on(buf, ss, rs):
-        for i in (1, 2):
+    def pass_own(buf, ss, rs):
+        gather_copy(buf, ss, rs, 1).wait_recv()
+        go(gather_copy(buf, ss, rs, 5))
+
+    def pass_other(buf, ss, rs):
+        gather_copy(buf, ss, rs, 4).wait_recv()
+        go(gather_copy(buf, ss, rs, 6))
+
+    def fanned(buf, ss, rs):
+        for i in (2, 3, 5, 6):
             gather_copy(buf, ss, rs, i).wait_recv()
-            go(gather_copy(buf, ss, rs, 2 + i))
-
-    def fanned(buf, ss, rs):
-        for i in (3, 4):
-            gather_copy(buf, ss, rs, i).wait_recv()
 
     def weight(n):
-        return w[n].reshape(D, UNIT)
+        return jnp.concatenate([w[n + i].reshape(D, TILE) for i in range(3)], axis=1)
 
     spread(SHARED)
 
@@ -421,25 +447,29 @@
     qi = lax.broadcasted_iota(jnp.int32, (T, T), 1)
     bias[...] = jnp.where((ki // 8) % 2 == (qi // 8) % 2, 0.0, -1e30).astype(F32)
     attend(spat, bias, probs, ft)
+    mixed_all[:, lanes(s)] = ft[...].astype(BF)
+    fan_own(mixed_all, mx_s, mx_r)
+    z_start(1)
+    z_start(2)
+    relay(SHARED)
     spread(0)
-    relay(SHARED)
-    mixed_all[:, lanes(s)] = ft[...].astype(BF)
     permute(ft, fp)
     t_to_rows(fp, rows_b, D)
+    loads[3].wait()
+    loads[4].wait()
     complete(SHARED)
     bias[...] = jnp.where(ki % 8 == qi % 8, 0.0, -1e30).astype(F32)
     rows_to_t(gout, cot, D)
+    pass_own(mixed_all, mx_s, mx_r)
+    relay(0)
     spread(1)
-    relay(0)
-    spread(2)
     x_relay()
     complete(0)
-    go(gather_copy(mixed_all, mx_s, mx_r, 0))
     both_cores(0)
 
     def hidden_body(n):
         tok = regroup(tokens[:, lanes(n, 384)].astype(F32))
-        acc = contract(rows_b[...], weight(n), 1, 0)
+        acc = contract(rows_b[...], weight(3 * n), 1, 0)
         hid[:, lanes(n, 384)] = (tok + acc).astype(BF)
 
     loop(3, hidden_body)
@@ -447,11 +477,12 @@
     hid_in[own, :] = hid[own, :]
     for k in range(1, NS):
         go(rows_copy(hid, hid_in, h_s, h_r, k))
+    fan_other(mixed_all, mx_s, mx_r)
+    spread(2)
     relay(1)
     x_complete()
     for k in range(1, NS):
         rows_copy(hid, hid_in, h_s, h_r, k).wait_recv()
-    fan_out(mixed_all, mx_s, mx_r)
 
     hf = hid_in[...].astype(F32)
     centred = hf - jnp.mean(hf, axis=-1, keepdims=True)
@@ -462,40 +493,42 @@
     rows_t[...] = (xh * sc[...] + sh[...]).astype(BF).astype(F32)
     rows_to_t(rows_t, ft, D)
     mod_all[:, lanes(s)] = ft[...].astype(BF)
-    go(gather_copy(mod_all, md_s, md_r, 0))
+    fan_own(mod_all, md_s, md_r)
     permute(ft, fp)
     t_to_rows(fp, rows_b, D)
+
+    def project(first, count):
+        def body(i):
+            acc = contract(rows_b[...], weight(first + 3 * i), 1, 0)
+            packed[rows8((first - 9) * TILE + 3 * TILE * i, 3 * TILE), :] = acc.astype(BF).astype(F32).T
+
+        loop(count, body)
+
+    pass_other(mixed_all, mx_s, mx_r)
     complete(1)
     relay(2)
-    fan_out(mod_all, md_s, md_r)
-
-    def project(first, count):
-        def body(i):
-            acc = contract(rows_b[...], weight(first + i), 1, 0)
-            packed[rows8((first - 3 + i) * UNIT, UNIT), :] = acc.astype(BF).astype(F32).T
-
-        loop(count, body)
-
     both_cores(SHARED)
-    project(6, 4)
+    project(9, 2)
     both_cores(1)
-    project(3, 3)
-    pass_on(mixed_all, mx_s, mx_r)
+    project(15, 4)
+    fan_other(mod_all, md_s, md_r)
+    attend(packed, bias, probs_t, None)
+    pass_own(mod_all, md_s, md_r)
     complete(2)
-    attend(packed, bias, probs_t, None)
     both_cores(2)
-    project(10, 2)
+    project(27, 3)
     attend_back(packed, probs_t, cot, grad)
     grad_b[...] = grad[...].astype(BF)
+    pass_other(mod_all, md_s, md_r)
     gt_all[:, lanes(s)] = grad_b[pl.ds(pl.multiple_of(s * 432, 16), 432), :]
 
     def weight_t(n, b):
-        return jnp.concatenate([w[n + i, b].reshape(576, UNIT) for i in range(3)], axis=1)
+        return jnp.concatenate([w[n + i, b].reshape(576, TILE) for i in range(9)], axis=1)
 
     def back_body(b):
         acc = jnp.zeros((576, T), F32)
         for q in range(3):
-            acc += contract(weight_t(3 + 3 * q, b), grad_b[pl.ds(q * D, D), :], 1, 0)
+            acc += contract(weight_t(9 + 9 * q, b), grad_b[pl.ds(q * D, D), :], 1, 0)
         fp[rows8(b * 576, 576), :] = acc
 
     loop(NC, back_body)
@@ -511,7 +544,6 @@
         go(rows_copy(g_out, g_in, g_s, g_r, k))
     for k in range(1, NS):
         go(cols_copy(grad_b, gt_all, 432, gt_s, gt_r, k))
-    pass_on(mod_all, md_s, md_r)
     for k in range(1, NS):
         rows_copy(g_out, g_in, g_s, g_r, k).wait_recv()
 
@@ -531,13 +563,7 @@
     loop(NC, mixed_body)
     unpermute(fp, ft)
 
-    attend_back(spat, probs, ft, grad)
-
-    def out_body(j):
-        out_tok[:, lanes(j)] = ungroup(g_in[:, lanes(j)].astype(F32)).astype(BF)
-
-    loop(9, out_body)
-
+    attend_back(spat, probs, ft, grad, 0, 8)
     fanned(mod_all, md_s, md_r)
     for k in range(1, NS):
         cols_copy(grad_b, gt_all, 432, gt_s, gt_r, k).wait_recv()
@@ -547,6 +573,8 @@
 
     loop(NY, gwi_body)
     go(sum_c(gwi_p, gwi_c, ri_s, ri_r))
+    attend_back(spat, probs, ft, grad, 8, 8)
+    add_c(gwi_p, gwi_c, gwi_h, gwi_y, ri_s, ri_r)
     fanned(mixed_all, mx_s, mx_r)
     for k in range(1, NS):
         cols_copy(gt_b, g_all, 144, gc_s, gc_r, k).wait_recv()
@@ -556,7 +584,11 @@
 
     loop(NY, gwo_body)
     go(sum_c(gwo_p, gwo_c, ro_s, ro_r))
-    add_c(gwi_p, gwi_c, gwi_h, gwi_y, ri_s, ri_r)
+
+    def out_body(j):
+        out_tok[:, lanes(j)] = ungroup(g_in[:, lanes(j)].astype(F32)).astype(BF)
+
+    loop(9, out_body)
     add_c(gwo_p, gwo_c, gwo_h, gwo_y, ro_s, ro_r)
 
     def qkv_body(j):
@@ -569,6 +601,11 @@
     add_z(gwo_t, gwo_z, ro_s, ro_r, out_gwo)
     for cp in started:
         cp.wait_send()
+
+
+def hand_over(*refs):
+    for src, dst in zip(refs[:4], refs[4:]):
+        dst[...] = src[...]
 
 
 def time_modulation(timesteps):
@@ -584,11 +621,11 @@
 
 def shards(qkv_spatial, tokens, timesteps, w_out, w_in, grad_out):
     sc, sh = time_modulation(timesteps)
-    tail = jnp.concatenate([w_out[MAIN:], w_in[MAIN:]], axis=1)
-    tail = tail.reshape(TAIL, 36, 128).transpose(1, 0, 2).reshape(144, 128)
     dma = lambda *n: DMA(n)
     scratch = [
-        VMEM((12, NC, NY, BLOCK, UNIT), BF),
+        VMEM((T, 3 * D), BF), VMEM((T, D), BF), VMEM((T, D), BF),
+        VMEM((SHARD, D), BF), VMEM((SHARD, 3 * D), BF), VMEM((144, 128), BF),
+        VMEM((36, NC, NY, BLOCK, TILE), BF),
         VMEM((NZ, 144, 128), BF),
         VMEM((3 * D, T), F32),
         VMEM((3 * D, T), F32),
@@ -615,13 +652,13 @@
         VMEM((D, T), BF),
         *[VMEM(n + (m,), BF) for m in (432, 144)
           for n in ((NY, 288), (NY, 144), (NY, 144), (3, 144), (4, 48), (4, 48))],
-        dma(4, 3), dma(4, 3), dma(3), dma(3), dma(4, 4), dma(4, 4), dma(4), dma(4), dma(4, 4), dma(4, 4),
-        dma(5), dma(5), dma(5), dma(5),
+        dma(5), dma(4, 3), dma(4, 3), dma(3), dma(3), dma(4, 4), dma(4, 4), dma(4), dma(4), dma(4, 4), dma(4, 4),
+        dma(7), dma(7), dma(7), dma(7),
         dma(7), dma(7), dma(7), dma(7), dma(7), dma(7), dma(7), dma(7),
         dma(8), dma(8), dma(8), dma(8),
     ]
     spec = pl.BlockSpec(memory_space=VMEM)
-    gq, gt, gwo, gwi = pl.pallas_call(
+    results = pl.pallas_call(
         kernel,
         out_shape=(
             jax.ShapeDtypeStruct((T, 3 * D), BF),
@@ -629,7 +666,7 @@
             jax.ShapeDtypeStruct((SHARD, 144), F32),
             jax.ShapeDtypeStruct((SHARD, 432), F32),
         ),
-        in_specs=[spec] * 8,
+        in_specs=[pl.BlockSpec(memory_space=pl.ANY)] * 5 + [spec] * 2,
         out_specs=(spec,) * 4,
         scratch_shapes=scratch,
         compiler_params=pltpu.CompilerParams(
@@ -637,8 +674,14 @@
         ),
     )(
         qkv_spatial.reshape(T, 3 * D), tokens.reshape(T, D), grad_out.reshape(T, D),
-        w_out, w_in, tail, sc, sh,
+        w_out, w_in, sc, sh,
     )
+    gq, gt, gwo, gwi = pl.pallas_call(
+        hand_over,
+        out_shape=tuple(jax.ShapeDtypeStruct(r.shape, r.dtype) for r in results),
+        in_specs=[spec] * 4,
+        out_specs=(spec,) * 4,
+    )(*results)
     return gq.reshape(qkv_spatial.shape), gt.reshape(tokens.shape), gwo, gwi
 
 

time: 149 us -> 128 us (0.86); the launches traced: 149 us -> 126 us
  Pallas kernels: 141 us -> 124 us
  local copies, waits for them, and re-layouts: 5.91 us -> 0.01 us
    pallas_call x1, Pallas kernels: 141 us -> 122 us  [shards(): pl.pallas_call(kernel, out_shape=(jax.ShapeDtypeStruct((T, 3 * D), BF), j...]
    unnamed x10 -> x0, local copies, waits for them, and re-layouts: 4.5 us -> none
    pallas_call x0 -> x1, Pallas kernels: none -> 2.33 us  [shards(): pl.pallas_call(hand_over, out_shape=tuple((jax.ShapeDtypeStruct(r.shape,...]
where the time goes in v4:
time: 128 us; the launch traced here: 126 us
  Pallas kernels  124 us (97%)
  between operations  1.31 us (1%)
    pallas_call x1, Pallas kernels, shards(): pl.pallas_call(kernel, out_shape=(jax.ShapeDtypeStruct((T, 3 * D), BF), j...  122 us

profile of v4, /device:TPU:1, one launch (start us, length us, event | category | flops | bytes accessed | tf_op | source)
XLA Modules:
  0.0 126.4 jit_solution(2431064264521259607)
XLA Ops:
  1.4 0.7 maximum_multiply_fusion.1
  2.0 122.0 %shard_map.93 = (bf16[128,3456]{1,0:T(8,128)(2,1)}, bf16[128,1152]{1,0:T(8,128)(2,1)}, f32[36,144]{1,0:T(8,128)}, f32[36,432]{1,0:T(8,128)}) custom-call(bf16[128,3456]{1,0:T(8,128)(2,1)} %bitcast.6, bf16[128,1152]{1,0:T(8,128)(2,1)} %bitcast.7, bf16[128,1152]{1,0:T(8,128)(2,1)} %bitcast.8, bf16[36,1152]{1,0:T(8,128)(2,1)} %wo_h.1, bf16[36,3456]{1,0:T(8,128)(2,1)} %wi_h.1, ...), custom_call_target="tpu_custom_call" | custom-call | tf_op jit(solution)/shard_map/pallas_call | solution.py:661
  124.0 2.3 %shard_map.94 = (bf16[128,3456]{1,0:T(8,128)(2,1)}, bf16[128,1152]{1,0:T(8,128)(2,1)}, f32[36,144]{1,0:T(8,128)}, f32[36,432]{1,0:T(8,128)}) custom-call(bf16[128,3456]{1,0:T(8,128)(2,1)} %get-tuple-element.12.refs_0_, bf16[128,1152]{1,0:T(8,128)(2,1)} %get-tuple-element.13.refs_1_, f32[36,144]{1,0:T(8,128)} %get-tuple-element.14.refs_2_, ...), custom_call_target="tpu_custom_call" | custom-call | tf_op jit(solution)/shard_map/pallas_call | solution.py:679
  (3 shorter events, 0.1 us)

commit v5 on v4

--- a/solution.py
+++ b/solution.py
@@ -103,8 +103,9 @@
     return [ref[rows8(D * i + HEAD * h, HEAD), :].astype(BF) for i in range(3)]
 
 
-def attend(packed, bias, probs, out):
+def attend(packed, bias, probs, out, first=0, count=HEADS):
     def body(h):
+        h = h + first // GROUP
         for hh in [GROUP * h + i for i in range(GROUP)]:
             q = packed[rows8(HEAD * hh, HEAD), :].astype(BF)
             k = packed[rows8(D + HEAD * hh, HEAD), :].astype(BF)
@@ -117,7 +118,7 @@
                 o = contract(v, p.astype(BF), 1, 0)
                 out[rows8(HEAD * hh, HEAD), :] = o.astype(BF).astype(F32)
 
-    loop(HEADS // GROUP, body)
+    loop(count // GROUP, body)
 
 
 def attend_back(packed, probs, cot, grad, first=0, count=HEADS):
@@ -144,7 +145,7 @@
     qkv_h, tokens_h, gout_h, wo_h, wi_h, sc, sh,
     out_qkv, out_tok, out_gwo, out_gwi,
     qkv, tokens, gout, wo, wi, tail, w, tails, packed, spat, probs, probs_t, bias, grad, grad_b, ft, fp, rows_b, rows_t, hid, hid_in, g_out,
-    xhat, rstd, mixed_all, mod_all, gt_all, g_all, cot, g_in, gt_b,
+    xhat, rstd, mixed_all, mod_all, gt_all, g_all, cot, g_in, gt_b, gp_b, swap,
     gwi_p, gwi_c, gwi_h, gwi_y, gwi_t, gwi_z, gwo_p, gwo_c, gwo_h, gwo_y, gwo_t, gwo_z,
     in_s, z_s, z_r, t_s, t_r, y_s, y_r, x_s, x_r, c_s, c_r, mx_s, mx_r, md_s, md_r,
     h_s, h_r, g_s, g_r, gt_s, gt_r, gc_s, gc_r, ri_s, ri_r, ro_s, ro_r,
@@ -247,9 +248,20 @@
     other = s + 1 - 2 * zl
 
     def gather_copy(buf, ss, rs, i):
-        slot = (s, s, s, other, other, 2 * lax.rem(x + 3, NX) + zl, 2 * lax.rem(x + 1, NX) + 1 - zl)[i]
+        slot = s
+        if i in (3, 4):
+            slot = other
+        if i == 5:
+            slot = 2 * lax.rem(x + 3, NX) + zl
+        if i == 6:
+            slot = 2 * lax.rem(x + 1, NX) + 1 - zl
+        rows = pl.ds(0, D)
+        if i in (1, 2):
+            rows = pl.ds(0, D // 2)
+        if i in (7, 8):
+            rows = pl.ds(D // 2, D // 2)
         to = pair if i == 0 else x_peer(1 if i % 2 == 1 else 3)
-        part = buf.at[:, lanes(slot)]
+        part = buf.at[rows, lanes(slot)]
         return copy(part, part, ss.at[i], rs.at[i], to)
 
     def rows_copy(src, dst, ss, rs, k):
@@ -349,6 +361,19 @@
     z_start(SHARED)
     z_start(0)
 
+    ki = lax.broadcasted_iota(jnp.int32, (T, T), 0)
+    qi = lax.broadcasted_iota(jnp.int32, (T, T), 1)
+    bias[...] = jnp.where((ki // 8) % 2 == (qi // 8) % 2, 0.0, -1e30).astype(F32)
+
+    def half_attention(i):
+        half = pl.ds(i * (D // 2), D // 2)
+        attend(spat, bias, probs, ft, 8 * i, 8)
+        mixed_all[half, lanes(s)] = ft[half, :].astype(BF)
+        for j in (1, 2):
+            go(gather_copy(mixed_all, mx_s, mx_r, j + 6 * i))
+
+    half_attention(0)
+
     for k in range(1, NZ):
         t_copy(k).wait_recv()
 
@@ -418,7 +443,7 @@
             c_copy(q, i).wait_recv()
 
     def fan_own(buf, ss, rs):
-        for i in (0, 1, 2):
+        for i in (0, 1, 2, 7, 8):
             go(gather_copy(buf, ss, rs, i))
 
     def fan_other(buf, ss, rs):
@@ -427,7 +452,8 @@
             go(gather_copy(buf, ss, rs, i))
 
     def pass_own(buf, ss, rs):
-        gather_copy(buf, ss, rs, 1).wait_recv()
+        for i in (1, 7):
+            gather_copy(buf, ss, rs, i).wait_recv()
         go(gather_copy(buf, ss, rs, 5))
 
     def pass_other(buf, ss, rs):
@@ -435,7 +461,7 @@
         go(gather_copy(buf, ss, rs, 6))
 
     def fanned(buf, ss, rs):
-        for i in (2, 3, 5, 6):
+        for i in (2, 8, 3, 5, 6):
             gather_copy(buf, ss, rs, i).wait_recv()
 
     def weight(n):
@@ -443,14 +469,10 @@
 
     spread(SHARED)
 
-    ki = lax.broadcasted_iota(jnp.int32, (T, T), 0)
-    qi = lax.broadcasted_iota(jnp.int32, (T, T), 1)
-    bias[...] = jnp.where((ki // 8) % 2 == (qi // 8) % 2, 0.0, -1e30).astype(F32)
-    attend(spat, bias, probs, ft)
-    mixed_all[:, lanes(s)] = ft[...].astype(BF)
-    fan_own(mixed_all, mx_s, mx_r)
+    half_attention(1)
     z_start(1)
     z_start(2)
+    go(gather_copy(mixed_all, mx_s, mx_r, 0))
     relay(SHARED)
     spread(0)
     permute(ft, fp)
@@ -461,6 +483,14 @@
     bias[...] = jnp.where(ki % 8 == qi % 8, 0.0, -1e30).astype(F32)
     rows_to_t(gout, cot, D)
     pass_own(mixed_all, mx_s, mx_r)
+
+    def swap_body(i):
+        row = lax.broadcasted_iota(jnp.int32, (T, NS * T), 0) + i * T
+        col = lax.broadcasted_iota(jnp.int32, (T, NS * T), 1)
+        want = (((col >> 4) & 7) << 7) | ((col >> 7) << 4) | (col & 15)
+        swap[rows8(i * T, T), :] = jnp.where(row == want, 1.0, 0.0).astype(BF)
+
+    loop(NS, swap_body)
     relay(0)
     spread(1)
     x_relay()
@@ -504,7 +534,6 @@
 
         loop(count, body)
 
-    pass_other(mixed_all, mx_s, mx_r)
     complete(1)
     relay(2)
     both_cores(SHARED)
@@ -517,10 +546,12 @@
     complete(2)
     both_cores(2)
     project(27, 3)
+    pass_other(mod_all, md_s, md_r)
     attend_back(packed, probs_t, cot, grad)
     grad_b[...] = grad[...].astype(BF)
-    pass_other(mod_all, md_s, md_r)
     gt_all[:, lanes(s)] = grad_b[pl.ds(pl.multiple_of(s * 432, 16), 432), :]
+    for k in range(1, NS):
+        go(cols_copy(grad_b, gt_all, 432, gt_s, gt_r, k))
 
     def weight_t(n, b):
         return jnp.concatenate([w[n + i, b].reshape(576, TILE) for i in range(9)], axis=1)
@@ -542,28 +573,12 @@
     g_in[own, :] = g_out[own, :]
     for k in range(1, NS):
         go(rows_copy(g_out, g_in, g_s, g_r, k))
+    pass_other(mixed_all, mx_s, mx_r)
+    rows_to_t(g_out, gp_b, D)
+    g_all[:, lanes(s)] = gp_b[pl.ds(pl.multiple_of(s * 144, 16), 144), :]
     for k in range(1, NS):
-        go(cols_copy(grad_b, gt_all, 432, gt_s, gt_r, k))
-    for k in range(1, NS):
-        rows_copy(g_out, g_in, g_s, g_r, k).wait_recv()
-
-    def tok_body(j):
-        gt_b[rows8(j * 128, 128), :] = g_in[:, lanes(j)].astype(F32).T.astype(BF)
-
-    loop(9, tok_body)
-    g_all[:, lanes(s)] = gt_b[pl.ds(pl.multiple_of(s * 144, 16), 144), :]
-    for k in range(1, NS):
-        go(cols_copy(gt_b, g_all, 144, gc_s, gc_r, k))
-
-    def mixed_body(b):
-        fp[rows8(b * 576, 576), :] = contract(
-            weight_t(0, b), gt_b[...], 1, 0
-        )
-
-    loop(NC, mixed_body)
-    unpermute(fp, ft)
-
-    attend_back(spat, probs, ft, grad, 0, 8)
+        go(cols_copy(gp_b, g_all, 144, gc_s, gc_r, k))
+
     fanned(mod_all, md_s, md_r)
     for k in range(1, NS):
         cols_copy(grad_b, gt_all, 432, gt_s, gt_r, k).wait_recv()
@@ -573,30 +588,44 @@
 
     loop(NY, gwi_body)
     go(sum_c(gwi_p, gwi_c, ri_s, ri_r))
-    attend_back(spat, probs, ft, grad, 8, 8)
+
+    for k in range(1, NS):
+        rows_copy(g_out, g_in, g_s, g_r, k).wait_recv()
+    rows_to_t(g_in, gt_b, D)
+
+    def mixed_body(b):
+        fp[rows8(b * 576, 576), :] = contract(weight_t(0, b), gt_b[...], 1, 0)
+
+    loop(NC, mixed_body)
+    unpermute(fp, ft)
     add_c(gwi_p, gwi_c, gwi_h, gwi_y, ri_s, ri_r)
+
     fanned(mixed_all, mx_s, mx_r)
     for k in range(1, NS):
-        cols_copy(gt_b, g_all, 144, gc_s, gc_r, k).wait_recv()
+        cols_copy(gp_b, g_all, 144, gc_s, gc_r, k).wait_recv()
+    g_sorted = contract(g_all[...], swap[...], 1, 0).astype(BF)
+    g_all[...] = g_sorted
 
     def gwo_body(b):
         gwo_p[b] = contract(mixed_all[rows8(b * 288, 288), :], g_all[...], 1, 1).astype(BF)
 
     loop(NY, gwo_body)
     go(sum_c(gwo_p, gwo_c, ro_s, ro_r))
+    attend_back(spat, probs, ft, grad, 0, 8)
+    add_c(gwo_p, gwo_c, gwo_h, gwo_y, ro_s, ro_r)
+    attend_back(spat, probs, ft, grad, 8, 8)
+    add_y(gwi_h, gwi_y, gwi_t, gwi_z, ri_s, ri_r)
+
+    def qkv_body(j):
+        out_qkv[:, lanes(j)] = ungroup(grad[rows8(j * 128, 128), :].T).astype(BF)
+
+    loop(27, qkv_body)
+    add_y(gwo_h, gwo_y, gwo_t, gwo_z, ro_s, ro_r)
 
     def out_body(j):
         out_tok[:, lanes(j)] = ungroup(g_in[:, lanes(j)].astype(F32)).astype(BF)
 
     loop(9, out_body)
-    add_c(gwo_p, gwo_c, gwo_h, gwo_y, ro_s, ro_r)
-
-    def qkv_body(j):
-        out_qkv[:, lanes(j)] = ungroup(grad[rows8(j * 128, 128), :].T).astype(BF)
-
-    loop(27, qkv_body)
-    add_y(gwi_h, gwi_y, gwi_t, gwi_z, ri_s, ri_r)
-    add_y(gwo_h, gwo_y, gwo_t, gwo_z, ro_s, ro_r)
     add_z(gwi_t, gwi_z, ri_s, ri_r, out_gwi)
     add_z(gwo_t, gwo_z, ro_s, ro_r, out_gwo)
     for cp in started:
@@ -650,10 +679,12 @@
         VMEM((D, T), F32),
         VMEM((T, D), BF),
         VMEM((D, T), BF),
+        VMEM((D, T), BF),
+        VMEM((NS * T, NS * T), BF),
         *[VMEM(n + (m,), BF) for m in (432, 144)
           for n in ((NY, 288), (NY, 144), (NY, 144), (3, 144), (4, 48), (4, 48))],
         dma(5), dma(4, 3), dma(4, 3), dma(3), dma(3), dma(4, 4), dma(4, 4), dma(4), dma(4), dma(4, 4), dma(4, 4),
-        dma(7), dma(7), dma(7), dma(7),
+        dma(9), dma(9), dma(9), dma(9),
         dma(7), dma(7), dma(7), dma(7), dma(7), dma(7), dma(7), dma(7),
         dma(8), dma(8), dma(8), dma(8),
     ]

time: 128 us -> 122 us (0.953); the launches traced: 126 us -> 122 us
  Pallas kernels: 124 us -> 120 us
    pallas_call x1, Pallas kernels: 122 us -> 118 us  [shards(): pl.pallas_call(kernel, out_shape=(jax.ShapeDtypeStruct((T, 3 * D), BF), j...]
where the time goes in v5:
time: 122 us
  Pallas kernels  120 us (98%)
  between operations  1.31 us (1%)
    pallas_call x1, Pallas kernels, shards(): pl.pallas_call(kernel, out_shape=(jax.ShapeDtypeStruct((T, 3 * D), BF), j...  118 us

profile of v5, /device:TPU:1, one launch (start us, length us, event | category | flops | bytes accessed | tf_op | source)
XLA Modules:
  0.0 122.1 jit_solution(809949829220564138)
XLA Ops:
  1.4 0.7 maximum_multiply_fusion.1
  2.0 117.8 %shard_map.93 = (bf16[128,3456]{1,0:T(8,128)(2,1)}, bf16[128,1152]{1,0:T(8,128)(2,1)}, f32[36,144]{1,0:T(8,128)}, f32[36,432]{1,0:T(8,128)}) custom-call(bf16[128,3456]{1,0:T(8,128)(2,1)} %bitcast.6, bf16[128,1152]{1,0:T(8,128)(2,1)} %bitcast.7, bf16[128,1152]{1,0:T(8,128)(2,1)} %bitcast.8, bf16[36,1152]{1,0:T(8,128)(2,1)} %wo_h.1, bf16[36,3456]{1,0:T(8,128)(2,1)} %wi_h.1, ...), custom_call_target="tpu_custom_call" | custom-call | tf_op jit(solution)/shard_map/pallas_call | solution.py:692
  119.8 2.3 %shard_map.94 = (bf16[128,3456]{1,0:T(8,128)(2,1)}, bf16[128,1152]{1,0:T(8,128)(2,1)}, f32[36,144]{1,0:T(8,128)}, f32[36,432]{1,0:T(8,128)}) custom-call(bf16[128,3456]{1,0:T(8,128)(2,1)} %get-tuple-element.12.refs_0_, bf16[128,1152]{1,0:T(8,128)(2,1)} %get-tuple-element.13.refs_1_, f32[36,144]{1,0:T(8,128)} %get-tuple-element.14.refs_2_, ...), custom_call_target="tpu_custom_call" | custom-call | tf_op jit(solution)/shard_map/pallas_call | solution.py:710
  (3 shorter events, 0.1 us)

commit v6 on v5

--- a/solution.py
+++ b/solution.py
@@ -11,7 +11,7 @@
 HEADS = 16
 D = 1152
 HEAD = D // HEADS
-GROUP = 4
+GROUP = 8
 T = 128
 NY, NZ, NC, NS = 4, 4, 2, 8
 NX = 4
@@ -146,9 +146,9 @@
     out_qkv, out_tok, out_gwo, out_gwi,
     qkv, tokens, gout, wo, wi, tail, w, tails, packed, spat, probs, probs_t, bias, grad, grad_b, ft, fp, rows_b, rows_t, hid, hid_in, g_out,
     xhat, rstd, mixed_all, mod_all, gt_all, g_all, cot, g_in, gt_b, gp_b, swap,
-    gwi_p, gwi_c, gwi_h, gwi_y, gwi_t, gwi_z, gwo_p, gwo_c, gwo_h, gwo_y, gwo_t, gwo_z,
+    gwa_p, gwa_c, gwa_h, gwa_y, gwa_t, gwa_z, gwb_p, gwb_c, gwb_h, gwb_y, gwb_t, gwb_z, gwo_p, gwo_c, gwo_h, gwo_y, gwo_t, gwo_z,
     in_s, z_s, z_r, t_s, t_r, y_s, y_r, x_s, x_r, c_s, c_r, mx_s, mx_r, md_s, md_r,
-    h_s, h_r, g_s, g_r, gt_s, gt_r, gc_s, gc_r, ri_s, ri_r, ro_s, ro_r,
+    h_s, h_r, g_s, g_r, gt_s, gt_r, gc_s, gc_r, ra_s, ra_r, rb_s, rb_r, ro_s, ro_r,
 ):
     d = lax.axis_index("dp")
     s = lax.axis_index("seq")
@@ -542,16 +542,16 @@
     project(15, 4)
     fan_other(mod_all, md_s, md_r)
     attend(packed, bias, probs_t, None)
-    pass_own(mod_all, md_s, md_r)
     complete(2)
     both_cores(2)
     project(27, 3)
-    pass_other(mod_all, md_s, md_r)
+    pass_own(mod_all, md_s, md_r)
     attend_back(packed, probs_t, cot, grad)
     grad_b[...] = grad[...].astype(BF)
     gt_all[:, lanes(s)] = grad_b[pl.ds(pl.multiple_of(s * 432, 16), 432), :]
     for k in range(1, NS):
         go(cols_copy(grad_b, gt_all, 432, gt_s, gt_r, k))
+    pass_other(mod_all, md_s, md_r)
 
     def weight_t(n, b):
         return jnp.concatenate([w[n + i, b].reshape(576, TILE) for i in range(9)], axis=1)
@@ -583,11 +583,16 @@
     for k in range(1, NS):
         cols_copy(grad_b, gt_all, 432, gt_s, gt_r, k).wait_recv()
 
-    def gwi_body(b):
-        gwi_p[b] = contract(mod_all[rows8(b * 288, 288), :], gt_all[...], 1, 1).astype(BF)
-
-    loop(NY, gwi_body)
-    go(sum_c(gwi_p, gwi_c, ri_s, ri_r))
+    def gwi_part(part, first, count):
+        def body(b):
+            part[b] = contract(mod_all[rows8(b * 288, 288), :], gt_all[pl.ds(first, count), :], 1, 1).astype(BF)
+
+        loop(NY, body)
+
+    gwi_part(gwa_p, 0, 256)
+    go(sum_c(gwa_p, gwa_c, ra_s, ra_r))
+    gwi_part(gwb_p, 256, 176)
+    go(sum_c(gwb_p, gwb_c, rb_s, rb_r))
 
     for k in range(1, NS):
         rows_copy(g_out, g_in, g_s, g_r, k).wait_recv()
@@ -598,7 +603,8 @@
 
     loop(NC, mixed_body)
     unpermute(fp, ft)
-    add_c(gwi_p, gwi_c, gwi_h, gwi_y, ri_s, ri_r)
+    add_c(gwa_p, gwa_c, gwa_h, gwa_y, ra_s, ra_r)
+    add_c(gwb_p, gwb_c, gwb_h, gwb_y, rb_s, rb_r)
 
     fanned(mixed_all, mx_s, mx_r)
     for k in range(1, NS):
@@ -613,8 +619,9 @@
     go(sum_c(gwo_p, gwo_c, ro_s, ro_r))
     attend_back(spat, probs, ft, grad, 0, 8)
     add_c(gwo_p, gwo_c, gwo_h, gwo_y, ro_s, ro_r)
+    add_y(gwa_h, gwa_y, gwa_t, gwa_z, ra_s, ra_r)
     attend_back(spat, probs, ft, grad, 8, 8)
-    add_y(gwi_h, gwi_y, gwi_t, gwi_z, ri_s, ri_r)
+    add_y(gwb_h, gwb_y, gwb_t, gwb_z, rb_s, rb_r)
 
     def qkv_body(j):
         out_qkv[:, lanes(j)] = ungroup(grad[rows8(j * 128, 128), :].T).astype(BF)
@@ -626,7 +633,8 @@
         out_tok[:, lanes(j)] = ungroup(g_in[:, lanes(j)].astype(F32)).astype(BF)
 
     loop(9, out_body)
-    add_z(gwi_t, gwi_z, ri_s, ri_r, out_gwi)
+    add_z(gwa_t, gwa_z, ra_s, ra_r, out_gwi.at[:, pl.ds(0, 256)])
+    add_z(gwb_t, gwb_z, rb_s, rb_r, out_gwi.at[:, pl.ds(256, 176)])
     add_z(gwo_t, gwo_z, ro_s, ro_r, out_gwo)
     for cp in started:
         cp.wait_send()
@@ -681,12 +689,12 @@
         VMEM((D, T), BF),
         VMEM((D, T), BF),
         VMEM((NS * T, NS * T), BF),
-        *[VMEM(n + (m,), BF) for m in (432, 144)
+        *[VMEM(n + (m,), BF) for m in (256, 176, 144)
           for n in ((NY, 288), (NY, 144), (NY, 144), (3, 144), (4, 48), (4, 48))],
         dma(5), dma(4, 3), dma(4, 3), dma(3), dma(3), dma(4, 4), dma(4, 4), dma(4), dma(4), dma(4, 4), dma(4, 4),
         dma(9), dma(9), dma(9), dma(9),
         dma(7), dma(7), dma(7), dma(7), dma(7), dma(7), dma(7), dma(7),
-        dma(8), dma(8), dma(8), dma(8),
+        dma(8), dma(8), dma(8), dma(8), dma(8), dma(8),
     ]
     spec = pl.BlockSpec(memory_space=VMEM)
     results = pl.pallas_call(

time: 122 us -> 120 us (0.984)
  Pallas kernels: 120 us -> 118 us
    pallas_call x1, Pallas kernels: 118 us -> 116 us  [shards(): pl.pallas_call(kernel, out_shape=(jax.ShapeDtypeStruct((T, 3 * D), BF), j...]
where the time goes in v6:
time: 120 us
  Pallas kernels  118 us (98%)
  between operations  1.31 us (1%)
    pallas_call x1, Pallas kernels, shards(): pl.pallas_call(kernel, out_shape=(jax.ShapeDtypeStruct((T, 3 * D), BF), j...  116 us

profile of v6, /device:TPU:1, one launch (start us, length us, event | category | flops | bytes accessed | tf_op | source)
XLA Modules:
  0.0 120.3 jit_solution(11780881749308078003)
XLA Ops:
  1.4 0.7 maximum_multiply_fusion.1
  2.0 116.0 %shard_map.93 = (bf16[128,3456]{1,0:T(8,128)(2,1)}, bf16[128,1152]{1,0:T(8,128)(2,1)}, f32[36,144]{1,0:T(8,128)}, f32[36,432]{1,0:T(8,128)}) custom-call(bf16[128,3456]{1,0:T(8,128)(2,1)} %bitcast.6, bf16[128,1152]{1,0:T(8,128)(2,1)} %bitcast.7, bf16[128,1152]{1,0:T(8,128)(2,1)} %bitcast.8, bf16[36,1152]{1,0:T(8,128)(2,1)} %wo_h.1, bf16[36,3456]{1,0:T(8,128)(2,1)} %wi_h.1, ...), custom_call_target="tpu_custom_call" | custom-call | tf_op jit(solution)/shard_map/pallas_call | solution.py:700
  118.0 2.3 %shard_map.94 = (bf16[128,3456]{1,0:T(8,128)(2,1)}, bf16[128,1152]{1,0:T(8,128)(2,1)}, f32[36,144]{1,0:T(8,128)}, f32[36,432]{1,0:T(8,128)}) custom-call(bf16[128,3456]{1,0:T(8,128)(2,1)} %get-tuple-element.12.refs_0_, bf16[128,1152]{1,0:T(8,128)(2,1)} %get-tuple-element.13.refs_1_, f32[36,144]{1,0:T(8,128)} %get-tuple-element.14.refs_2_, ...), custom_call_target="tpu_custom_call" | custom-call | tf_op jit(solution)/shard_map/pallas_call | solution.py:718
  (3 shorter events, 0.1 us)
